TPU v7x, 512 devices: a whole 4x4x16 slice. The times are simulated.
512 devices in a mesh: dp: 8 (over y, core), center: 64 (over x, z).
Axes of the slice: x: 4, y: 4, z: 16, core: 2. Of those that a mesh axis runs over, the one named last changes fastest.
Arguments:
- points: bfloat16 [65536, 256], P(('dp', 'center')), may hold values from -93 to 93, as said below
- centers: bfloat16 [65536, 256], P('center'), may hold values from -4 to 4, as said below
- picks: int32 [32768], P(('dp', 'center')), may hold values from 0 to 127
Outputs:
- new_centers: bfloat16 [65536, 256], P('center')
- mass: float32 [65536], P('center')
Inputs may be any that keep to these rules, and one draw needn't show every extreme that they name: `points`: real values, with rows of unlike scale. `centers`: real values of order one.
All inputs are finite; a program needn't handle non-finite values.
Results may differ from a plain program's by a relative error of at most 0.0031.
Values may be sent and summed in bfloat16 or wider, within the bound.
No kernel may reach another device: no remote copies, remote signals or barrier semaphores. Data moves between devices by JAX's collectives and lax.ppermute only.
A program may use at most 64 MiB of HBM per device.

v0:
```python
import math

import jax
import jax.numpy as jnp
from jax import lax
from jax.sharding import PartitionSpec as P

sigma_sq = 8.0


def block_size(count):
    return math.gcd(count, 512)


def scores_of(rows, centers, half_norm):
    dots = jnp.einsum("rw,kw->rk", rows, centers, preferred_element_type=jnp.float32)
    return (dots - half_norm) / sigma_sq


def row_stats(rows, centers, half_norm):
    count = rows.shape[0]
    block = block_size(count)
    blocks = rows.reshape(count // block, block, rows.shape[1])

    def row_one_block(part):
        score = scores_of(part, centers, half_norm)
        top = jnp.max(score, axis=1)
        total = jnp.sum(jnp.exp(score - top[:, None]), axis=1)
        return (top, total)

    tops, totals = lax.map(row_one_block, blocks)
    return (tops.reshape(count), totals.reshape(count))


def accumulate(carry, rows, tops, totals, centers, half_norm):
    count = rows.shape[0]
    block = block_size(count)
    blocks = rows.reshape(count // block, block, rows.shape[1])
    top_blocks = tops.reshape(count // block, block)
    total_blocks = totals.reshape(count // block, block)

    def accumulate_one_block(state, items):
        part, top, total = items
        weighted, counts = state
        score = scores_of(part, centers, half_norm)
        resp = jnp.exp(score - top[:, None]) / total[:, None]
        resp_low = resp.astype(jnp.bfloat16)
        weighted = weighted + jnp.einsum(
            "rk,rw->kw", resp_low, part, preferred_element_type=jnp.float32
        )
        counts = counts + jnp.sum(resp, axis=0)
        return ((weighted, counts), None)

    state, _ = lax.scan(accumulate_one_block, carry, (blocks, top_blocks, total_blocks))
    return state


def body(points, centers, picks):
    local_rows = jnp.take(points, picks, axis=0)
    centers_f = centers.astype(jnp.float32)
    half_norm = 0.5 * jnp.sum(centers_f * centers_f, axis=1)
    local_count = centers.shape[0]
    width = centers.shape[1]
    init = (jnp.zeros((local_count, width), jnp.float32), jnp.zeros((local_count,), jnp.float32))
    gathered = lax.all_gather(local_rows, "center", axis=0, tiled=True)
    tops, totals = row_stats(gathered, centers, half_norm)
    glob_top = lax.pmax(tops, "center")
    glob_total = lax.psum(totals * jnp.exp(tops - glob_top), "center")
    weighted, counts = accumulate(init, gathered, glob_top, glob_total, centers, half_norm)
    weighted, counts = lax.psum((weighted, counts), "dp")
    new_centers = ((weighted + centers_f) / (counts[:, None] + 1.0)).astype(jnp.bfloat16)
    return (new_centers, counts)


def solution(mesh):
    return jax.shard_map(
        body,
        mesh=mesh,
        in_specs=(P(("dp", "center"), None), P("center", None), P(("dp", "center"))),
        out_specs=(P("center", None), P("center")),
        check_vma=False,
    )
```

profile of v0, /device:TPU:1, one launch (start us, length us, event | category | flops | bytes accessed | tf_op | source)
XLA Modules:
  0.0 833.7 jit_solution(7879774231766045079)
XLA Ops:
  7.2 0.7 compare_select_fusion
  7.9 0.7 compare_and_fusion
  8.6 0.7 gather_fusion
  9.3 0.7 broadcast_select_fusion
  10.1 1.3 fusion.12
  11.3 137.6 %all-gather.2.cloned.1.call-done = bf16[4096,256]{1,0:T(8,128)(2,1)} async-done(((bf16[64,256]{1,0:T(8,128)(2,1)}), bf16[4096,256]{1,0:T(8,128)(2,1)}) %all-gather.2.cloned.1.call-update) | async-done | bytes 2097168 | tf_op jit(solution)/shard_map/all_gather | solution.py:65
  149.0 19.4 %while.25 = (s32[]{:T(128)}, f32[8,512]{1,0:T(8,128)S(1)}, f32[8,512]{1,0:T(8,128)S(1)}, bf16[8,512,256]{2,1,0:T(8,128)(2,1)}, bf16[1024,256]{1,0:T(8,128)(2,1)}, /*index=5*/f32[1024]{0:T(1024)S(1)}, s32[]{:T(128)}, s32[]{:T(128)}) while((s32[]{:T(128)}, f32[8,512]{1,0:T(8,128)S(1)}, f32[8,512]{1,0:T(8,128)S(1)}, ...), condition=%wide.region_4.5_spmd, body=%wide.region_1.0_spmd.sunk | while | flops 272104448 | bytes 5003869 | solution.py:31
  149.0 1.7 fusion.26
  150.6 0.6 exponential_reduce_fusion.2
  151.3 0.1 dynamic_update_slice.9
  151.4 1.7 fusion.26
  153.1 0.6 exponential_reduce_fusion.2
  153.8 1.7 fusion.26
  155.5 0.6 exponential_reduce_fusion.2
  156.1 0.1 dynamic_update_slice.9
  156.2 1.7 fusion.26
  157.9 0.6 exponential_reduce_fusion.2
  158.6 1.7 fusion.26
  160.3 0.6 exponential_reduce_fusion.2
  161.1 1.7 fusion.26
  162.8 0.6 exponential_reduce_fusion.2
  163.5 1.7 fusion.26
  165.2 0.6 exponential_reduce_fusion.2
  165.9 1.7 fusion.26
  167.6 0.6 exponential_reduce_fusion.2
  168.4 220.9 %pmax.7 = f32[4096]{0:T(1024)S(1)} all-reduce(f32[4096]{0:T(1024)S(1)} %bitcast.47), channel_id=1, replica_groups=mesh['dp'=8,'center'=64] {'center'}, use_global_device_ids=true, to_apply=%region_5.6 | all-reduce | flops 4096 | bytes 32768 | tf_op jit(solution)/shard_map/pmax | solution.py:67
  389.3 219.6 %psum.21 = f32[8,512]{1,0:T(8,128)S(1)} all-reduce(f32[8,512]{1,0:T(8,128)S(1)} %reshape.38), channel_id=1, replica_groups=mesh['dp'=8,'center'=64] {'center'}, use_global_device_ids=true, to_apply=%region_6.7 | all-reduce | flops 4096 | bytes 32768 | tf_op jit(solution)/shard_map/psum | solution.py:68
  608.9 29.7 %while.26 = (s32[]{:T(128)}, f32[1024,256]{1,0:T(8,128)S(1)}, f32[1024]{0:T(1024)S(1)}, bf16[8,512,256]{2,1,0:T(8,128)(2,1)}, bf16[1024,256]{1,0:T(8,128)(2,1)},...) while((s32[]{:T(128)}, f32[1024,256]{1,0:T(8,128)S(1)}, ...), condition=%wide.region_9.10_spmd.clone, body=%wide.region_7.9_spmd.clone.sunk | while | flops 540541952 | bytes 5276788 | solution.py:54
  608.9 1.9 fusion.30
  610.8 1.8 convolution_add_fusion.2
  612.6 1.9 fusion.30
  614.5 1.8 convolution_add_fusion.2
  616.4 1.9 fusion.30
  618.3 1.8 convolution_add_fusion.2
  620.1 1.9 fusion.30
  622.0 1.8 convolution_add_fusion.2
  623.8 1.9 fusion.30
  625.7 1.8 convolution_add_fusion.2
  627.5 1.9 fusion.30
  629.4 1.8 convolution_add_fusion.2
  631.2 1.9 fusion.30
  633.1 1.8 convolution_add_fusion.2
  635.0 1.9 fusion.30
  636.8 1.8 convolution_add_fusion.2
  638.7 1.0 copy-done.1
  639.7 132.2 %psum.23 = f32[1024]{0:T(1024)S(1)} all-reduce(f32[1024]{0:T(1024)S(1)} %get-tuple-element.81), channel_id=1, replica_groups=mesh['dp'=8,'center'=64] {'dp'}, use_global_device_ids=true, to_apply=%region_11.12 | all-reduce | flops 1024 | bytes 8192 | tf_op jit(solution)/shard_map/psum | solution.py:70
  771.9 52.5 %all-reduce.2.cloned.1.call-done = f32[1024,256]{1,0:T(8,128)} async-done(((f32[1024,256]{1,0:T(8,128)}), f32[1024,256]{1,0:T(8,128)}) %all-reduce.2.cloned.1.call-update) | async-done | bytes 1048592 | tf_op jit(solution)/shard_map/psum | solution.py:70
  824.5 2.4 fusion.14
  (51 shorter events, 1.1 us)
Async XLA Ops:
  7.2 1.4 copy-start
  7.2 141.8 %all-gather.2.cloned.1.call-start = ((), (), s32[]{:S(2)}) async-start(), calls=%async_computation | async-start | bytes 2129920 | tf_op jit(solution)/shard_map/all_gather | solution.py:65
  10.0 814.5 %all-reduce.2.cloned.1.call-start = ((), (), s32[]{:S(2)}) async-start(), calls=%async_computation.1 | async-start | bytes 2097152 | tf_op jit(solution)/shard_map/psum | solution.py:70
  638.7 1.0 copy-start.1
  771.9 54.9 %copy-start.2 = (f32[1024]{0:T(1024)}, f32[1024]{0:T(1024)S(1)}, u32[]{:S(2)}) copy-start(f32[1024]{0:T(1024)S(1)} %psum.23) | copy-start | bytes 12292
Sparse Core Ops, SparseCore 0:
  11.5 137.3 all-gather.1
  639.8 184.5 all-reduce.1
where the time goes:
time: 835 us; the launch traced here: 834 us
  blocking collectives  573 us (69%)
  waiting for transfers between devices  190 us (23%)
  matrix products  42.7 us (5%)
  between operations  14.2 us (2%)
  other arithmetic  10.5 us (1%)
    pmax x1, blocking collectives, body(): glob_top = lax.pmax(tops, 'center')  221 us
    psum x1, blocking collectives, body(): glob_total = lax.psum(totals * jnp.exp(tops - glob_top), 'center')  220 us
    all_gather x1, waiting for transfers between devices, body(): gathered = lax.all_gather(local_rows, 'center', axis=0, tiled=True)  138 us
    psum x1, blocking collectives, body(): weighted, counts = lax.psum((weighted, counts), 'dp')  132 us
    psum x1, waiting for transfers between devices, body(): weighted, counts = lax.psum((weighted, counts), 'dp')  52.5 us
    dot_general x16, matrix products, scores_of(): jnp.einsum('rw,kw->rk', rows, centers, preferred_element_type=jnp.float32)  28.4 us
  transfers between devices with their start and end apart: 2, of which 2 were waited for; matrix products, arithmetic and copies ran while one was open for 0% of the time, Pallas kernels for 0%

commit v1 on v0

v1 whole, which is shorter than its diff:
```python
import functools

import jax
import jax.numpy as jnp
from jax import lax
from jax.experimental import pallas as pl
from jax.experimental.pallas import tpu as pltpu
from jax.sharding import Mesh, PartitionSpec as P

WIDTH = 256
SUB = 256
BLOCK = 1024
LANES = 128
F32 = jnp.float32
BF16 = jnp.bfloat16


def prepare_centers(c_ref, cs_ref, hn_ref):
    c = c_ref[...].astype(F32)
    norm = jnp.sum(c * c, axis=1, keepdims=True) * (1.0 / 16.0)
    hn_ref[...] = jnp.broadcast_to(norm, hn_ref.shape)
    cs_ref[...] = (c * 0.125).astype(BF16)


def scores(cs, hn, rows):
    dots = lax.dot_general(cs, rows, (((1,), (1,)), ((), ())), preferred_element_type=F32)
    return dots - jnp.concatenate([hn] * (rows.shape[0] // LANES), axis=1)


def stats_kernel(rows_ref, c_ref, l_ref, cs_ref, hn_ref):
    @pl.when(pl.program_id(0) == 0)
    def _():
        prepare_centers(c_ref, cs_ref, hn_ref)

    for j in range(BLOCK // SUB):
        s = scores(cs_ref[...], hn_ref[...], rows_ref[j * SUB : (j + 1) * SUB, :])
        top = jnp.max(s, axis=0, keepdims=True)
        lse = top + jnp.log(jnp.sum(jnp.exp(s - top), axis=0, keepdims=True))
        for i in range(SUB // LANES):
            k = j * (SUB // LANES) + i
            l_ref[k : k + 1, :] = lse[:, i * LANES : (i + 1) * LANES]


def row_stats(rows, centers):
    count, k = rows.shape[0], centers.shape[0]
    return pl.pallas_call(
        stats_kernel,
        grid=(count // BLOCK,),
        in_specs=[
            pl.BlockSpec((BLOCK, WIDTH), lambda i: (i, 0)),
            pl.BlockSpec((k, WIDTH), lambda i: (0, 0)),
        ],
        out_specs=pl.BlockSpec((BLOCK // LANES, LANES), lambda i: (i, 0)),
        out_shape=jax.ShapeDtypeStruct((count // LANES, LANES), F32),
        scratch_shapes=[pltpu.VMEM((k, WIDTH), BF16), pltpu.VMEM((k, LANES), F32)],
        compiler_params=pltpu.CompilerParams(vmem_limit_bytes=40 * 2**20),
        name="row_stats",
    )(rows, centers)


def sums_kernel(parts, rows_ref, c_ref, l_ref, out_ref, cs_ref, hn_ref, acc_ref, mass_ref):
    step = pl.program_id(0)

    @pl.when(step == 0)
    def _():
        prepare_centers(c_ref, cs_ref, hn_ref)
        acc_ref[...] = jnp.zeros_like(acc_ref)
        mass_ref[...] = jnp.zeros_like(mass_ref)

    for j in range(BLOCK // SUB):
        rows = rows_ref[j * SUB : (j + 1) * SUB, :]
        s = scores(cs_ref[...], hn_ref[...], rows)
        n = SUB // LANES
        lse = jnp.concatenate([l_ref[j * n + i : j * n + i + 1, :] for i in range(n)], axis=1)
        resp = jnp.exp(s - lse)
        total = resp[:, :LANES]
        for i in range(1, n):
            total = total + resp[:, i * LANES : (i + 1) * LANES]
        mass_ref[...] += total
        acc_ref[...] += jnp.dot(resp.astype(BF16), rows, preferred_element_type=F32)

    @pl.when(step == pl.num_programs(0) - 1)
    def _():
        k = acc_ref.shape[0] // parts
        out_ref[:, k:, :] = jnp.zeros((parts, 8, WIDTH), F32)
        for p in range(parts):
            out_ref[p, :k, :] = acc_ref[p * k : (p + 1) * k, :]
            mass = jnp.sum(jnp.transpose(mass_ref[p * k : (p + 1) * k, :]), axis=0, keepdims=True)
            lane = (p % 2) * LANES
            for q in range(parts):
                out_ref[q, k + p // 2 : k + p // 2 + 1, lane : lane + LANES] = mass
            out_ref[p, k + 4 : k + 5, :LANES] = mass


def row_sums(rows, centers, lse, parts):
    count, k = rows.shape[0], centers.shape[0]
    out = (parts, k // parts + 8, WIDTH)
    return pl.pallas_call(
        functools.partial(sums_kernel, parts),
        grid=(count // BLOCK,),
        in_specs=[
            pl.BlockSpec((BLOCK, WIDTH), lambda i: (i, 0)),
            pl.BlockSpec((k, WIDTH), lambda i: (0, 0)),
            pl.BlockSpec((BLOCK // LANES, LANES), lambda i: (i, 0)),
        ],
        out_specs=pl.BlockSpec(out, lambda i: (0, 0, 0)),
        out_shape=jax.ShapeDtypeStruct(out, F32),
        scratch_shapes=[
            pltpu.VMEM((k, WIDTH), BF16),
            pltpu.VMEM((k, LANES), F32),
            pltpu.VMEM((k, WIDTH), F32),
            pltpu.VMEM((k, LANES), F32),
        ],
        compiler_params=pltpu.CompilerParams(vmem_limit_bytes=40 * 2**20),
        name="row_sums",
    )(rows, centers, lse)


def finish_kernel(got_ref, c_ref, new_ref, mass_ref):
    k = c_ref.shape[0]
    total = got_ref[0]
    for i in range(1, got_ref.shape[0]):
        total = total + got_ref[i]
    mass_ref[...] = total[k : k + 4, :]
    own = jnp.transpose(jnp.broadcast_to(total[k + 4 : k + 5, :LANES], (LANES, k)))
    own = jnp.concatenate([own] * (WIDTH // LANES), axis=1)
    new_ref[...] = ((total[:k, :] + c_ref[...].astype(F32)) / (own + 1.0)).astype(BF16)


def finish(got, centers):
    k = centers.shape[0]
    return pl.pallas_call(
        finish_kernel,
        out_shape=(
            jax.ShapeDtypeStruct((k, WIDTH), BF16),
            jax.ShapeDtypeStruct((4, WIDTH), F32),
        ),
        compiler_params=pltpu.CompilerParams(vmem_limit_bytes=40 * 2**20),
        name="finish",
    )(got, centers)


def everyone(value, axes, count):
    sent = jnp.broadcast_to(value[None], (count,) + value.shape)
    return lax.all_to_all(sent, axes, 0, 0, tiled=True)


def merge(parts):
    top = jnp.max(parts, axis=0)
    return top + jnp.log(jnp.sum(jnp.exp(parts - top[None]), axis=0))


def body(points, centers, picks):
    chosen = (picks[:, None] == lax.iota(jnp.int32, points.shape[0])[None, :]).astype(BF16)
    rows = jnp.dot(chosen, points, preferred_element_type=F32).astype(BF16)
    rows = everyone(rows, "zh", 4).reshape(-1, WIDTH)
    rows = everyone(rows, "zl", 4).reshape(-1, WIDTH)
    rows = everyone(rows, "x", 4).reshape(-1, WIDTH)
    lse = row_stats(rows, centers)
    lse = merge(everyone(lse, ("x", "zl"), 16))
    lse = merge(everyone(lse, "zh", 4))
    sums = row_sums(rows, centers, lse, 8)
    got = lax.all_to_all(sums, ("y", "core"), 0, 0, tiled=True)
    part = lax.axis_index("y") * 2 + lax.axis_index("core")
    k = centers.shape[0] // 8
    new, mass = finish(got, lax.dynamic_slice_in_dim(centers, part * k, k, 0))
    new = lax.all_gather(new, ("y", "core"), axis=0, tiled=True)
    return (new, mass.reshape(-1))


def solution(mesh):
    axes = ("y", "core", "x", "zh", "zl")
    fine = Mesh(mesh.devices.reshape(4, 2, 4, 4, 4), axes)
    return jax.shard_map(
        body,
        mesh=fine,
        in_specs=(P(axes, None), P(axes[2:], None), P(axes)),
        out_specs=(P(axes[2:], None), P(axes[2:])),
        check_vma=False,
    )
```

time: 835 us -> 159 us (0.19)
  blocking collectives: 573 us -> 115 us
  waiting for transfers between devices: 190 us -> 15.8 us
  matrix products: 42.7 us -> 0.84 us
  Pallas kernels: 0 us -> 13.9 us
  between operations: 14.2 us -> 0.73 us
  other arithmetic: 10.5 us -> 0.12 us
  starting transfers between devices: 0.08 us -> 9.86 us
    psum x2 -> x0, blocking collectives: 352 us -> none  [the longest x1 220 us: body(): glob_total = lax.psum(totals * jnp.exp(tops - glob_top), 'center')]
    pmax x1 -> x0, blocking collectives: 221 us -> none  [body(): glob_top = lax.pmax(tops, 'center')]
    all_gather x1 -> x0, waiting for transfers between devices: 138 us -> none  [body(): gathered = lax.all_gather(local_rows, 'center', axis=0, tiled=True)]
    all_to_all x0 -> x5, blocking collectives: none -> 101 us  [everyone(): return lax.all_to_all(sent, axes, 0, 0, tiled=True)]
    psum x1 -> x0, waiting for transfers between devices: 52.5 us -> none  [body(): weighted, counts = lax.psum((weighted, counts), 'dp')]
    dot_general x24 -> x1, matrix products: 42.7 us -> 0.84 us  [body(): rows = jnp.dot(chosen, points, preferred_element_type=F32).astype(BF16)]
    all_to_all x0 -> x1, waiting for transfers between devices: none -> 15.8 us  [body(): got = lax.all_to_all(sums, ('y', 'core'), 0, 0, tiled=True)]
    pallas_call x0 -> x3, Pallas kernels: none -> 13.9 us  [the longest x1 7.85 us: row_sums(): pl.pallas_call(functools.partial(sums_kernel, parts), grid=(count // BLOC...]
  transfers between devices with their start and end apart: 2 -> 1, of which waited for: 2 -> 1; matrix products, arithmetic and copies ran while one was open for 0% -> 0% of each run, Pallas kernels for 0% -> 0%
where the time goes in v1:
time: 159 us
  blocking collectives  115 us (72%)
  waiting for transfers between devices  15.8 us (10%)
  Pallas kernels  13.9 us (9%)
  starting transfers between devices  9.86 us (6%)
  local copies, waits for them, and re-layouts  2.45 us (2%)
    all_to_all x5, blocking collectives, everyone(): return lax.all_to_all(sent, axes, 0, 0, tiled=True)  101 us
    all_to_all x1, waiting for transfers between devices, body(): got = lax.all_to_all(sums, ('y', 'core'), 0, 0, tiled=True)  15.8 us
    all_gather x1, blocking collectives, body(): new = lax.all_gather(new, ('y', 'core'), axis=0, tiled=True)  13.8 us
    all_to_all x1, starting transfers between devices, body(): got = lax.all_to_all(sums, ('y', 'core'), 0, 0, tiled=True)  9.86 us
    pallas_call x1, Pallas kernels, row_sums(): pl.pallas_call(functools.partial(sums_kernel, parts), grid=(count // BLOC...  7.85 us
    pallas_call x1, Pallas kernels, row_stats(): pl.pallas_call(stats_kernel, grid=(count // BLOCK,), in_specs=[pl.BlockSp...  5.92 us
  transfers between devices with their start and end apart: 1, of which 1 were waited for; matrix products, arithmetic and copies ran while one was open for 0% of the time, Pallas kernels for 0%

profile of v1, /device:TPU:1, one launch (start us, length us, event | category | flops | bytes accessed | tf_op | source)
XLA Modules:
  0.0 159.0 jit_solution(15264006017122836096)
XLA Ops:
  0.6 0.0 copy-start
  0.6 0.8 copy-done
  1.5 0.8 convolution_convert_fusion
  2.3 28.1 %all_to_all.30 = bf16[4,64,256]{2,1,0:T(8,128)(2,1)S(1)} all-to-all(bf16[4,64,256]{2,1,0:T(8,128)(2,1)S(1)} %broadcast_in_dim.14), channel_id=1, replica_groups=mesh['y'=4,'core'=2,'x'=4,'zh'=4,'zl'=4] {'zh'}, dimensions={0} | all-to-all | bytes 262144 | tf_op jit(solution)/shard_map/all_to_all | solution.py:145
  30.5 16.5 %all_to_all.31 = bf16[4,256,256]{2,1,0:T(8,128)(2,1)S(1)} all-to-all(bf16[4,256,256]{2,1,0:T(8,128)(2,1)S(1)} %broadcast_in_dim.16), channel_id=1, replica_groups=mesh['y'=4,'core'=2,'x'=4,'zh'=4,'zl'=4] {'zl'}, dimensions={0} | all-to-all | bytes 1048576 | tf_op jit(solution)/shard_map/all_to_all | solution.py:145
  46.9 0.1 broadcast_in_dim.18
  47.1 0.0 copy-start.1
  47.1 27.9 %all_to_all.32 = bf16[4,1024,256]{2,1,0:T(8,128)(2,1)S(1)} all-to-all(bf16[4,1024,256]{2,1,0:T(8,128)(2,1)S(1)} %broadcast_in_dim.18), channel_id=1, replica_groups=mesh['y'=4,'core'=2,'x'=4,'zh'=4,'zl'=4] {'x'}, dimensions={0} | all-to-all | bytes 4194304 | tf_op jit(solution)/shard_map/all_to_all | solution.py:145
  75.0 0.0 copy-done.1
  75.0 5.9 %row_stats.1 = f32[32,128]{1,0:T(8,128)S(1)} custom-call(bf16[4096,256]{1,0:T(8,128)(2,1)S(1)} %bitcast.6, bf16[1024,256]{1,0:T(8,128)(2,1)S(1)} %copy-done.1), custom_call_target="tpu_custom_call" | custom-call | tf_op jit(solution)/shard_map/row_stats/pallas_call | solution.py:46
  81.0 11.3 %all_to_all.33 = f32[16,32,128]{2,1,0:T(8,128)S(1)} all-to-all(f32[16,32,128]{2,1,0:T(8,128)S(1)} %broadcast_in_dim.19), channel_id=1, replica_groups=mesh['y'=4,'core'=2,'x'=4,'zh'=4,'zl'=4] {'x','zl'}, dimensions={0} | all-to-all | bytes 524288 | tf_op jit(solution)/shard_map/all_to_all | solution.py:145
  92.3 0.1 exponential_reduce_fusion
  92.4 17.7 %all_to_all.34 = f32[4,32,128]{2,1,0:T(8,128)S(1)} all-to-all(f32[4,32,128]{2,1,0:T(8,128)S(1)} %broadcast_in_dim.20), channel_id=1, replica_groups=mesh['y'=4,'core'=2,'x'=4,'zh'=4,'zl'=4] {'zh'}, dimensions={0} | all-to-all | bytes 131072 | tf_op jit(solution)/shard_map/all_to_all | solution.py:145
  110.1 7.9 %row_sums.1 = f32[8,136,256]{2,1,0:T(8,128)} custom-call(bf16[4096,256]{1,0:T(8,128)(2,1)S(1)} %bitcast.7, bf16[1024,256]{1,0:T(8,128)(2,1)S(1)} %copy-done.1, f32[32,128]{1,0:T(8,128)S(1)} %log_add_fusion.l_ref), custom_call_target="tpu_custom_call" | custom-call | tf_op jit(solution)/shard_map/row_sums/pallas_call | solution.py:98
  118.0 9.9 %all-to-all-start.5 = ((f32[8,136,256]{2,1,0:T(8,128)}), f32[8,136,256]{2,1,0:T(8,128)S(1)}, u32[]{:S(2)}, u32[]{:S(2)}) async-start(f32[8,136,256]{2,1,0:T(8,128)} %row_sums.1), calls=%async_computation.5 | async-start | bytes 2228224 | tf_op jit(solution)/shard_map/all_to_all | solution.py:163
  127.8 15.8 %all-to-all-done.5.got_ref = f32[8,136,256]{2,1,0:T(8,128)S(1)} async-done(((f32[8,136,256]{2,1,0:T(8,128)}), f32[8,136,256]{2,1,0:T(8,128)S(1)}, u32[]{:S(2)}, u32[]{:S(2)}) %all-to-all-start.5) | async-done | bytes 1114144 | tf_op jit(solution)/shard_map/all_to_all | solution.py:163
  143.6 0.1 finish.1
  143.8 13.8 %all_gather.3 = bf16[1024,256]{1,0:T(8,128)(2,1)S(1)} all-gather(bf16[128,256]{1,0:T(8,128)(2,1)S(1)} %get-tuple-element.4), channel_id=1, replica_groups=mesh['y'=4,'core'=2,'x'=4,'zh'=4,'zl'=4] {'y','core'}, dimensions={0}, use_global_device_ids=true | all-gather | bytes 589824 | tf_op jit(solution)/shard_map/all_gather | solution.py:167
  157.6 0.6 copy.5
  158.2 0.8 copy.7
  (10 shorter events, 0.1 us)
Async XLA Ops:
  0.6 0.8 copy-start
  47.1 27.9 %copy-start.1 = (bf16[1024,256]{1,0:T(8,128)(2,1)S(1)}, bf16[1024,256]{1,0:T(8,128)(2,1)}, u32[]{:S(2)}) copy-start(bf16[1024,256]{1,0:T(8,128)(2,1)} %c_ref.3) | copy-start | bytes 1572868
  118.0 25.7 %all-to-all-start.5 = ((f32[8,136,256]{2,1,0:T(8,128)}), f32[8,136,256]{2,1,0:T(8,128)S(1)}, u32[]{:S(2)}, u32[]{:S(2)}) async-start(f32[8,136,256]{2,1,0:T(8,128)} %row_sums.1), calls=%async_computation.5 | async-start | bytes 2228224 | tf_op jit(solution)/shard_map/all_to_all | solution.py:163

commit v2 on v0

v2 whole, which is shorter than its diff:
```python
import functools

import jax
import jax.numpy as jnp
from jax import lax
from jax.experimental import pallas as pl
from jax.experimental.pallas import tpu as pltpu
from jax.sharding import Mesh, PartitionSpec as P

WIDTH = 256
SUB = 256
LANES = 128
F32 = jnp.float32
BF16 = jnp.bfloat16
AXES = ("y", "core", "x", "zh", "zl")
GROUP = ("core", "x", "zh", "zl")
PARAMS = pltpu.CompilerParams(vmem_limit_bytes=40 * 2**20)


def place(core, x, z):
    return (core * 4 + x) * 16 + z


def mixed_groups():
    along_z = [[place(0, x, 4 * h + i) for i in range(4)] for x in range(4) for h in range(4)]
    along_x = [[place(1, i, z) for i in range(4)] for z in range(16)]
    return along_z + along_x


def mixed_moves(d):
    moves = []
    for x in range(4):
        for z in range(16):
            dz = -d if d == 2 and z % 2 else d
            moves.append((place(0, x, z), place(0, (x + d) % 4, z)))
            moves.append((place(1, x, z), place(1, x, (z + dz) % 16)))
    return moves


def cost(rows, centers, dots):
    return pl.CostEstimate(
        flops=2 * dots * rows * centers * WIDTH,
        bytes_accessed=2 * WIDTH * (rows + centers),
        transcendentals=rows * centers,
    )


def prepared(c):
    c = c.astype(F32)
    norm = jnp.sum(c * c, axis=1, keepdims=True) * (1.0 / 16.0)
    return (c * 0.125).astype(BF16), jnp.broadcast_to(norm, (c.shape[0], LANES))


def scores(cs, hn, rows):
    dots = lax.dot_general(cs, rows, (((1,), (1,)), ((), ())), preferred_element_type=F32)
    return dots - jnp.concatenate([hn] * (rows.shape[0] // LANES), axis=1)


def piece_stats(rows_ref, c_ref, cs_ref, hn_ref):
    cs_ref[...], hn_ref[...] = prepared(c_ref[...])
    out = []
    for j in range(rows_ref.shape[0] // SUB):
        s = scores(cs_ref[...], hn_ref[...], rows_ref[j * SUB : (j + 1) * SUB, :])
        top = jnp.max(s, axis=0, keepdims=True)
        lse = top + jnp.log(jnp.sum(jnp.exp(s - top), axis=0, keepdims=True))
        out += [lse[:, i * LANES : (i + 1) * LANES] for i in range(SUB // LANES)]
    return jnp.concatenate(out, axis=0)


def center_scratch(k):
    return [pltpu.VMEM((k, WIDTH), BF16), pltpu.VMEM((k, LANES), F32)]


def stats_kernel(rows_ref, c_ref, l_ref, cs_ref, hn_ref):
    l_ref[...] = piece_stats(rows_ref, c_ref, cs_ref, hn_ref)


def row_stats(rows, centers):
    n, k = rows.shape[0], centers.shape[0]
    return pl.pallas_call(
        stats_kernel,
        out_shape=jax.ShapeDtypeStruct((n // LANES, LANES), F32),
        scratch_shapes=center_scratch(k),
        compiler_params=PARAMS,
        cost_estimate=cost(n, k, 1),
        name="row_stats",
    )(rows, centers)


def piece_at(me, d):
    return pl.multiple_of(((me + 4 - d) % 4) * 8, 8)


def last_kernel(me_ref, r2_ref, c_ref, l0_ref, l1_ref, l3_ref, out_ref, cs_ref, hn_ref):
    l2 = piece_stats(r2_ref, c_ref, cs_ref, hn_ref)
    pieces = (l0_ref[...], l1_ref[...], l2, l3_ref[...])
    me = me_ref[0]
    for copy in range(out_ref.shape[0]):
        for d in range(4):
            out_ref[copy, pl.ds(piece_at(me, d), 8), :] = pieces[d]


def last_stats(me, r2, centers, l0, l1, l3, copies):
    n = 4 * r2.shape[0]
    smem, vmem = pl.BlockSpec(memory_space=pltpu.SMEM), pl.BlockSpec(memory_space=pltpu.VMEM)
    return pl.pallas_call(
        last_kernel,
        in_specs=[smem] + [vmem] * 5,
        out_shape=jax.ShapeDtypeStruct((copies, n // LANES, LANES), F32),
        scratch_shapes=center_scratch(centers.shape[0]),
        compiler_params=PARAMS,
        cost_estimate=cost(r2.shape[0], centers.shape[0], 1),
        name="last_stats",
    )(me, r2, centers, l0, l1, l3)


def merged(parts_ref):
    top = parts_ref[0]
    for i in range(1, parts_ref.shape[0]):
        top = jnp.maximum(top, parts_ref[i])
    total = jnp.exp(parts_ref[0] - top)
    for i in range(1, parts_ref.shape[0]):
        total = total + jnp.exp(parts_ref[i] - top)
    return top + jnp.log(total)


def merge_kernel(parts_ref, out_ref):
    out_ref[...] = jnp.broadcast_to(merged(parts_ref)[None], out_ref.shape)


def merge(parts, copies):
    return pl.pallas_call(
        merge_kernel,
        out_shape=jax.ShapeDtypeStruct((copies,) + parts.shape[1:], F32),
        compiler_params=PARAMS,
        name="merge",
    )(parts)


def sums_kernel(parts, me_ref, half_ref, r0, r1, r2, r3, c_ref, parts_ref, out_ref, mass_ref, l_ref, cs_ref, hn_ref):
    half, k = out_ref.shape[0] * (out_ref.shape[1] - 8), out_ref.shape[1] - 8
    start = pl.multiple_of(half_ref[0] * half, half)
    cs_ref[...], hn_ref[...] = prepared(c_ref[pl.ds(start, half), :])
    me, n = me_ref[0], SUB // LANES
    l_ref[...] = merged(parts_ref)
    first = True
    for d, ref in enumerate((r0, r1, r2, r3)):
        piece = l_ref[pl.ds(piece_at(me, d), 8), :]
        for j in range(ref.shape[0] // SUB):
            rows = ref[j * SUB : (j + 1) * SUB, :]
            at = j * n
            lse = jnp.concatenate([piece[at + i : at + i + 1, :] for i in range(n)], axis=1)
            resp = jnp.exp(scores(cs_ref[...], hn_ref[...], rows) - lse)
            mass = resp[:, :LANES]
            for i in range(1, n):
                mass = mass + resp[:, i * LANES : (i + 1) * LANES]
            sums = jnp.dot(resp.astype(BF16), rows, preferred_element_type=F32)
            if first:
                mass_ref[...] = mass
                for p in range(parts):
                    out_ref[p, :k, :] = sums[p * k : (p + 1) * k, :]
            else:
                mass_ref[...] += mass
                for p in range(parts):
                    out_ref[p, :k, :] += sums[p * k : (p + 1) * k, :]
            first = False

    out_ref[:, k:, :] = jnp.zeros((parts, 8, WIDTH), F32)
    for p in range(parts):
        mass = jnp.sum(jnp.transpose(mass_ref[p * k : (p + 1) * k, :]), axis=0, keepdims=True)
        lane = (p % 2) * LANES
        for q in range(parts):
            out_ref[q, k + p // 2 : k + p // 2 + 1, lane : lane + LANES] = mass
        out_ref[p, k + 2 : k + 3, :LANES] = mass


def half_sums(me, half, pieces, centers, stats, parts):
    k = centers.shape[0] // 2
    l = stats.shape[1:]
    smem, vmem = pl.BlockSpec(memory_space=pltpu.SMEM), pl.BlockSpec(memory_space=pltpu.VMEM)
    return pl.pallas_call(
        functools.partial(sums_kernel, parts),
        in_specs=[smem] * 2 + [vmem] * 6,
        out_shape=jax.ShapeDtypeStruct((parts, k // parts + 8, WIDTH), F32),
        scratch_shapes=[pltpu.VMEM((k, LANES), F32), pltpu.VMEM(l, F32)] + center_scratch(k),
        compiler_params=PARAMS,
        cost_estimate=cost(l[0] * LANES, k, 2),
        name="half_sums",
    )(me, half, *pieces, centers, stats)


def combine_kernel(y_ref, a_ref, b_ref, *out_refs):
    for d, out_ref in enumerate(out_refs):
        p = (y_ref[0] + d) % 4
        out_ref[...] = a_ref[p] + b_ref[p]


def combine(y, a, b):
    smem, vmem = pl.BlockSpec(memory_space=pltpu.SMEM), pl.BlockSpec(memory_space=pltpu.VMEM)
    return pl.pallas_call(
        combine_kernel,
        in_specs=[smem, vmem, vmem],
        out_shape=[jax.ShapeDtypeStruct(a.shape[1:], F32)] * a.shape[0],
        compiler_params=PARAMS,
        name="combine",
    )(y, a, b)


def finish_kernel(a_ref, b_ref, c_ref, d_ref, centers_ref, new_ref, mass_ref):
    k = centers_ref.shape[0]
    total = (a_ref[...] + b_ref[...]) + (c_ref[...] + d_ref[...])
    mass_ref[...] = total[k : k + 2, :]
    own = jnp.transpose(jnp.broadcast_to(total[k + 2 : k + 3, :LANES], (LANES, k)))
    own = jnp.concatenate([own] * (WIDTH // LANES), axis=1)
    new_ref[...] = ((total[:k, :] + centers_ref[...].astype(F32)) / (own + 1.0)).astype(BF16)


def finish(got, centers):
    k = centers.shape[0]
    return pl.pallas_call(
        finish_kernel,
        out_shape=(
            jax.ShapeDtypeStruct((k, WIDTH), BF16),
            jax.ShapeDtypeStruct((2, WIDTH), F32),
        ),
        compiler_params=PARAMS,
        name="finish",
    )(*got, centers)


def everyone(value, axes, count, groups=None):
    sent = jnp.broadcast_to(value[None], (count,) + value.shape)
    return lax.all_to_all(sent, axes, 0, 0, tiled=True, axis_index_groups=groups)


def around(value, axis, count, d):
    return lax.ppermute(value, axis, [(i, (i + d) % count) for i in range(count)])


def body(points, centers, picks):
    core = lax.axis_index("core").astype(jnp.int32).reshape(1)
    y = lax.axis_index("y").astype(jnp.int32).reshape(1)
    me = jnp.where(core == 0, lax.axis_index("x"), lax.axis_index("zl")).astype(jnp.int32)
    k = centers.shape[0] // 8
    mine = lax.dynamic_slice_in_dim(centers, (core[0] * 4 + y[0]) * k, k, 0)

    chosen = (picks[:, None] == lax.iota(jnp.int32, points.shape[0])[None, :]).astype(BF16)
    rows = jnp.dot(chosen, points, preferred_element_type=F32).astype(BF16)
    rows = everyone(rows, "zh", 4).reshape(-1, WIDTH)
    r0 = everyone(rows, GROUP, 4, mixed_groups()).reshape(-1, WIDTH)
    r2 = lax.ppermute(r0, GROUP, mixed_moves(2))
    r1 = lax.ppermute(r0, GROUP, mixed_moves(1))
    r3 = lax.ppermute(r0, GROUP, mixed_moves(-1))

    l0, l1, l3 = row_stats(r0, centers), row_stats(r1, centers), row_stats(r3, centers)
    stats = last_stats(me, r2, centers, l0, l1, l3, 4)
    stats = lax.all_to_all(stats, "x", 0, 0, tiled=True)
    stats = lax.all_to_all(merge(stats, 16), ("zh", "zl"), 0, 0, tiled=True)

    pieces = (r0, r1, r2, r3)
    theirs = half_sums(me, 1 - core, pieces, centers, stats, 4)
    theirs = around(theirs, "core", 2, 1)
    sums = combine(y, half_sums(me, core, pieces, centers, stats, 4), theirs)
    got = [sums[0]] + [around(sums[d], "y", 4, d) for d in (2, 1, 3)]
    new, mass = finish(got, mine)
    new = lax.all_gather(new, "y", axis=0, tiled=True)
    new = lax.all_gather(new, "core", axis=0, tiled=True)
    mass = lax.all_gather(mass, "core", axis=0, tiled=True)
    return (new, mass.reshape(-1))


def solution(mesh):
    fine = Mesh(mesh.devices.reshape(4, 2, 4, 4, 4), AXES)
    return jax.shard_map(
        body,
        mesh=fine,
        in_specs=(P(AXES, None), P(AXES[2:], None), P(AXES)),
        out_specs=(P(AXES[2:], None), P(AXES[2:])),
        check_vma=False,
    )
```

time: 835 us -> 141 us (0.17)
  blocking collectives: 573 us -> 63.6 us
  waiting for transfers between devices: 190 us -> 20.2 us
  matrix products: 42.7 us -> 0.84 us
  starting transfers between devices: 0.08 us -> 39.1 us
  between operations: 14.2 us -> 0.83 us
  Pallas kernels: 0 us -> 12.3 us
  other arithmetic: 10.5 us -> 0 us
    psum x2 -> x0, blocking collectives: 352 us -> none  [the longest x1 220 us: body(): glob_total = lax.psum(totals * jnp.exp(tops - glob_top), 'center')]
    pmax x1 -> x0, blocking collectives: 221 us -> none  [body(): glob_top = lax.pmax(tops, 'center')]
    all_gather x1 -> x0, waiting for transfers between devices: 138 us -> none  [body(): gathered = lax.all_gather(local_rows, 'center', axis=0, tiled=True)]
    psum x1 -> x0, waiting for transfers between devices: 52.5 us -> none  [body(): weighted, counts = lax.psum((weighted, counts), 'dp')]
    all_to_all x0 -> x3, blocking collectives: none -> 45.8 us  [the longest x2 39 us: everyone(): lax.all_to_all(sent, axes, 0, 0, tiled=True, axis_index_groups=groups)]
    dot_general x24 -> x1, matrix products: 42.7 us -> 0.84 us  [body(): rows = jnp.dot(chosen, points, preferred_element_type=F32).astype(BF16)]
    ppermute x0 -> x7, starting transfers between devices: none -> 32.2 us  [the longest x4 23 us: around(): lax.ppermute(value, axis, [(i, (i + d) % count) for i in range(count)])]
    all_gather x0 -> x3, blocking collectives: none -> 17.8 us  [the longest x1 10.1 us: body(): new = lax.all_gather(new, 'y', axis=0, tiled=True)]
  transfers between devices with their start and end apart: 2 -> 8, of which waited for: 2 -> 6; matrix products, arithmetic and copies ran while one was open for 0% -> 0% of each run, Pallas kernels for 0% -> 5%
where the time goes in v2:
time: 141 us; the launch traced here: 140 us
  blocking collectives  63.6 us (45%)
  starting transfers between devices  39.1 us (28%)
  waiting for transfers between devices  20.2 us (14%)
  Pallas kernels  12.3 us (9%)
  local copies, waits for them, and re-layouts  3.33 us (2%)
    all_to_all x2, blocking collectives, everyone(): lax.all_to_all(sent, axes, 0, 0, tiled=True, axis_index_groups=groups)  39 us
    ppermute x4, starting transfers between devices, around(): lax.ppermute(value, axis, [(i, (i + d) % count) for i in range(count)])  23 us
    all_to_all x1, waiting for transfers between devices, body(): stats = lax.all_to_all(merge(stats, 16), ('zh', 'zl'), 0, 0, tiled=True)  12.8 us
    all_gather x1, blocking collectives, body(): new = lax.all_gather(new, 'y', axis=0, tiled=True)  10.1 us
    all_to_all x1, starting transfers between devices, body(): stats = lax.all_to_all(merge(stats, 16), ('zh', 'zl'), 0, 0, tiled=True)  6.94 us
    all_to_all x1, blocking collectives, body(): stats = lax.all_to_all(stats, 'x', 0, 0, tiled=True)  6.84 us
    all_gather x1, blocking collectives, body(): new = lax.all_gather(new, 'core', axis=0, tiled=True)  5.84 us
    pallas_call x2, Pallas kernels, half_sums(): pl.pallas_call(functools.partial(sums_kernel, parts), in_specs=[smem] * 2...  5.65 us
  transfers between devices with their start and end apart: 8, of which 6 were waited for; matrix products, arithmetic and copies ran while one was open for 0% of the time, Pallas kernels for 5%

profile of v2, /device:TPU:1, one launch (start us, length us, event | category | flops | bytes accessed | tf_op | source)
XLA Modules:
  0.0 140.2 jit_solution(11375479856561796742)
XLA Ops:
  0.6 0.0 copy-start
  0.6 0.8 copy-done
  1.5 0.8 convolution_convert_fusion
  2.3 28.1 %all_to_all.20 = bf16[4,64,256]{2,1,0:T(8,128)(2,1)S(1)} all-to-all(bf16[4,64,256]{2,1,0:T(8,128)(2,1)S(1)} %broadcast_in_dim.25), channel_id=1, replica_groups=mesh['y'=4,'core'=2,'x'=4,'zh'=4,'zl'=4] {'zh'}, dimensions={0} | all-to-all | bytes 262144 | tf_op jit(solution)/shard_map/all_to_all | solution.py:233
  30.5 0.0 copy-start.1
  30.5 10.9 %all_to_all.21 = bf16[4,256,256]{2,1,0:T(8,128)(2,1)S(1)} all-to-all(bf16[4,256,256]{2,1,0:T(8,128)(2,1)S(1)} %broadcast_in_dim.27), channel_id=1, replica_groups={{0,1,2,3},{4,5,6,7},{8,9,10,11},{12,13,14,15},{16,17,18,19},{20,21,22,2..., dimensions={0} | all-to-all | bytes 1048576 | tf_op jit(solution)/shard_map/all_to_all | solution.py:233
  41.4 3.3 %collective-permute-start = (bf16[1024,256]{1,0:T(8,128)(2,1)S(1)}, bf16[1024,256]{1,0:T(8,128)(2,1)S(1)}, u32[]{:S(2)}, u32[]{:S(2)}) collective-permute-start(bf16[1024,256]{1,0:T(8,128)(2,1)S(1)} %bitcast.10), channel_id=1, source_target_pairs={{0,16},{64,65},{1,17},{65,66},{2,18},{66,67},{3,19},{67,68},{4,20}... | collective-permute-start | bytes 1572872 | tf_op jit(solution)/shard_map/ppermute | solution.py:252
  44.7 3.1 %collective-permute-start.2 = (bf16[1024,256]{1,0:T(8,128)(2,1)S(1)}, bf16[1024,256]{1,0:T(8,128)(2,1)S(1)}, u32[]{:S(2)}, u32[]{:S(2)}) collective-permute-start(bf16[1024,256]{1,0:T(8,128)(2,1)S(1)} %bitcast.11), channel_id=1, source_target_pairs={{0,48},{64,79},{1,49},{65,64},{2,50},{66,65},{3,51},{67,66},{4,52}... | collective-permute-start | bytes 1572872 | tf_op jit(solution)/shard_map/ppermute | solution.py:253
  47.9 2.7 %collective-permute-start.1 = (bf16[1024,256]{1,0:T(8,128)(2,1)S(1)}, bf16[1024,256]{1,0:T(8,128)(2,1)S(1)}, u32[]{:S(2)}, u32[]{:S(2)}) collective-permute-start(bf16[1024,256]{1,0:T(8,128)(2,1)S(1)} %bitcast.12), channel_id=1, source_target_pairs={{0,32},{64,66},{1,33},{65,79},{2,34},{66,68},{3,35},{67,65},{4,36}... | collective-permute-start | bytes 1572872 | tf_op jit(solution)/shard_map/ppermute | solution.py:251
  50.6 0.0 copy-done.1
  50.6 1.4 %row_stats.3.l0_ref = f32[8,128]{1,0:T(8,128)S(1)} custom-call(bf16[1024,256]{1,0:T(8,128)(2,1)S(1)} %bitcast.13, bf16[1024,256]{1,0:T(8,128)(2,1)S(1)} %copy-done.1), custom_call_target="tpu_custom_call" | custom-call | flops 536870912 | bytes 1048576 | tf_op jit(solution)/shard_map/row_stats/pallas_call | solution.py:80
  52.1 0.4 collective-permute-done.rows_ref.r1
  52.5 1.4 %row_stats.4.l1_ref = f32[8,128]{1,0:T(8,128)S(1)} custom-call(bf16[1024,256]{1,0:T(8,128)(2,1)S(1)} %collective-permute-done.rows_ref.r1, bf16[1024,256]{1,0:T(8,128)(2,1)S(1)} %copy-done.1), custom_call_target="tpu_custom_call" | custom-call | flops 536870912 | bytes 1048576 | tf_op jit(solution)/shard_map/row_stats/pallas_call | solution.py:80
  53.9 1.0 collective-permute-done.2.rows_ref.r3
  54.9 1.4 %row_stats.5.l3_ref = f32[8,128]{1,0:T(8,128)S(1)} custom-call(bf16[1024,256]{1,0:T(8,128)(2,1)S(1)} %collective-permute-done.2.rows_ref.r3, bf16[1024,256]{1,0:T(8,128)(2,1)S(1)} %copy-done.1), custom_call_target="tpu_custom_call" | custom-call | flops 536870912 | bytes 1048576 | tf_op jit(solution)/shard_map/row_stats/pallas_call | solution.py:80
  56.4 3.5 %collective-permute-done.1.r2_ref.r2 = bf16[1024,256]{1,0:T(8,128)(2,1)S(1)} collective-permute-done((bf16[1024,256]{1,0:T(8,128)(2,1)S(1)}, bf16[1024,256]{1,0:T(8,128)(2,1)S(1)}, u32[]{:S(2)}, u32[]{:S(2)}) %collective-permute-start.1) | collective-permute-done | bytes 524320 | tf_op jit(solution)/shard_map/ppermute | solution.py:251
  59.9 0.0 copy-start.2
  59.9 1.4 %last_stats.1 = f32[4,32,128]{2,1,0:T(8,128)S(1)} custom-call(s32[1]{0:T(128)S(6)} %select_n.7.me_ref, bf16[1024,256]{1,0:T(8,128)(2,1)S(1)} %collective-permute-done.1.r2_ref.r2, bf16[1024,256]{1,0:T(8,128)(2,1)S(1)} %copy-done.1, f32[8,128]{1,0:T(8,128)S(1)} %row_stats.3.l0_ref, f32[8,128]{1,0:T(8,128)S(1)} %row_stats.4.l1_ref, f32[8,128]{1,0:T(8,128)S(1)} %row_stats.5.l3_ref), custom_call_target="tpu_custom_call" | custom-call | flops 536870912 | bytes 1048576 | tf_op jit(solution)/shard_map/last_stats/pallas_call | solution.py:106
  61.3 0.0 copy-done.2
  61.3 6.8 %all_to_all.22.parts_ref = f32[4,32,128]{2,1,0:T(8,128)S(1)} all-to-all(f32[4,32,128]{2,1,0:T(8,128)S(1)} %last_stats.1), channel_id=1, replica_groups=mesh['y'=4,'core'=2,'x'=4,'zh'=4,'zl'=4] {'x'}, dimensions={0} | all-to-all | bytes 131072 | tf_op jit(solution)/shard_map/all_to_all | solution.py:257
  68.2 0.0 copy-start.3
  68.2 0.7 merge.1
  68.9 6.9 %all-to-all-start.3 = ((f32[16,32,128]{2,1,0:T(8,128)}), f32[16,32,128]{2,1,0:T(8,128)S(1)}, u32[]{:S(2)}, u32[]{:S(2)}) async-start(f32[16,32,128]{2,1,0:T(8,128)} %merge.1), calls=%async_computation.3 | async-start | bytes 524288 | tf_op jit(solution)/shard_map/all_to_all | solution.py:258
  75.9 12.8 %all-to-all-done.3.parts_ref = f32[16,32,128]{2,1,0:T(8,128)S(1)} async-done(((f32[16,32,128]{2,1,0:T(8,128)}), f32[16,32,128]{2,1,0:T(8,128)S(1)}, u32[]{:S(2)}, u32[]{:S(2)}) %all-to-all-start.3) | async-done | bytes 262176 | tf_op jit(solution)/shard_map/all_to_all | solution.py:258
  88.7 0.0 copy-done.3
  88.7 2.8 %half_sums.3 = f32[4,136,256]{2,1,0:T(8,128)S(1)} custom-call(s32[1]{0:T(128)S(6)} %select_n.7.me_ref, s32[1]{0:T(128)S(6)} %sub.3.half_ref, bf16[1024,256]{1,0:T(8,128)(2,1)S(1)} %bitcast.14, bf16[1024,256]{1,0:T(8,128)(2,1)S(1)} %collective-permute-done.rows_ref.r1, bf16[1024,256]{1,0:T(8,128)(2,1)S(1)} %copy-done.3, ...), custom_call_target="tpu_custom_call" | custom-call | flops 2147483648 | bytes 2359296 | tf_op jit(solution)/shard_map/half_sums/pallas_call | solution.py:181
  91.5 11.6 %collective-permute-start.3 = (f32[4,136,256]{2,1,0:T(8,128)S(1)}, f32[4,136,256]{2,1,0:T(8,128)S(1)}, u32[]{:S(2)}, u32[]{:S(2)}) collective-permute-start(f32[4,136,256]{2,1,0:T(8,128)S(1)} %half_sums.3), channel_id=1, source_target_pairs={{0,64},{64,0},{1,65},{65,1},{2,66},{66,2},{3,67},{67,3},{4,68},{68... | collective-permute-start | bytes 1671176 | tf_op jit(solution)/shard_map/ppermute | solution.py:237
  103.1 0.0 copy-start.4
  103.1 1.0 copy-done.4
  104.2 2.8 %half_sums.2.a_ref = f32[4,136,256]{2,1,0:T(8,128)S(1)} custom-call(s32[1]{0:T(128)S(6)} %select_n.7.me_ref, s32[1]{0:T(128)} %bitcast.1.half_ref, bf16[1024,256]{1,0:T(8,128)(2,1)S(1)} %bitcast.15, bf16[1024,256]{1,0:T(8,128)(2,1)S(1)} %collective-permute-done.rows_ref.r1, bf16[1024,256]{1,0:T(8,128)(2,1)S(1)} %copy-done.4, ...), custom_call_target="tpu_custom_call" | custom-call | flops 2147483648 | bytes 2359296 | tf_op jit(solution)/shard_map/half_sums/pallas_call | solution.py:181
  107.0 0.0 collective-permute-done.3.b_ref
  107.0 0.1 combine.1
  107.1 4.8 %collective-permute-start.4 = (f32[136,256]{1,0:T(8,128)S(1)}, f32[136,256]{1,0:T(8,128)S(1)}, u32[]{:S(2)}, u32[]{:S(2)}) collective-permute-start(f32[136,256]{1,0:T(8,128)S(1)} %get-tuple-element.9), channel_id=1, source_target_pairs={{0,256},{128,384},{256,0},{384,128},{1,257},{129,385},{257,1},{385... | collective-permute-start | bytes 417800 | tf_op jit(solution)/shard_map/ppermute | solution.py:237
  111.9 2.3 %collective-permute-start.5 = (f32[136,256]{1,0:T(8,128)S(1)}, f32[136,256]{1,0:T(8,128)S(1)}, u32[]{:S(2)}, u32[]{:S(2)}) collective-permute-start(f32[136,256]{1,0:T(8,128)S(1)} %get-tuple-element.10), channel_id=1, source_target_pairs={{0,128},{128,256},{256,384},{384,0},{1,129},{129,257},{257,385},{3... | collective-permute-start | bytes 417800 | tf_op jit(solution)/shard_map/ppermute | solution.py:237
  114.3 4.2 %collective-permute-start.6 = (f32[136,256]{1,0:T(8,128)S(1)}, f32[136,256]{1,0:T(8,128)S(1)}, u32[]{:S(2)}, u32[]{:S(2)}) collective-permute-start(f32[136,256]{1,0:T(8,128)S(1)} %get-tuple-element.11), channel_id=1, source_target_pairs={{0,384},{128,0},{256,128},{384,256},{1,385},{129,1},{257,129},{385... | collective-permute-start | bytes 417800 | tf_op jit(solution)/shard_map/ppermute | solution.py:237
  118.5 0.0 collective-permute-done.4.b_ref
  118.5 1.5 %collective-permute-done.5.c_ref = f32[136,256]{1,0:T(8,128)S(1)} collective-permute-done((f32[136,256]{1,0:T(8,128)S(1)}, f32[136,256]{1,0:T(8,128)S(1)}, u32[]{:S(2)}, u32[]{:S(2)}) %collective-permute-start.5) | collective-permute-done | bytes 139296 | tf_op jit(solution)/shard_map/ppermute | solution.py:237
  120.0 0.9 collective-permute-done.6.d_ref
  120.9 0.1 finish.1
  121.0 10.1 %all_gather.9 = bf16[512,256]{1,0:T(8,128)(2,1)S(1)} all-gather(bf16[128,256]{1,0:T(8,128)(2,1)S(1)} %get-tuple-element.12), channel_id=1, replica_groups=mesh['y'=4,'core'=2,'x'=4,'zh'=4,'zl'=4] {'y'}, dimensions={0}, use_global_device_ids=true | all-gather | bytes 327680 | tf_op jit(solution)/shard_map/all_gather | solution.py:266
  131.1 5.8 %all_gather.10 = bf16[1024,256]{1,0:T(8,128)(2,1)S(1)} all-gather(bf16[512,256]{1,0:T(8,128)(2,1)S(1)} %all_gather.9), channel_id=1, replica_groups=mesh['y'=4,'core'=2,'x'=4,'zh'=4,'zl'=4] {'core'}, dimensions={0}, use_global_device_ids=true | all-gather | bytes 786432 | tf_op jit(solution)/shard_map/all_gather | solution.py:267
  137.0 1.8 %all-gather = f32[2,2,256]{2,1,0:T(2,128)S(1)} all-gather(f32[1,2,256]{2,1,0:T(2,128)S(1)} %bitcast.16), channel_id=1, replica_groups=mesh['y'=4,'core'=2,'x'=4,'zh'=4,'zl'=4] {'core'}, dimensions={0}, use_global_device_ids=true | all-gather | bytes 6144 | tf_op jit(solution)/shard_map/all_gather | solution.py:268
  138.8 0.6 copy.5
  139.4 0.8 copy.7
  (3 shorter events, 0.1 us)
Async XLA Ops:
  0.6 0.8 copy-start
  30.5 20.1 %copy-start.1 = (bf16[1024,256]{1,0:T(8,128)(2,1)S(1)}, bf16[1024,256]{1,0:T(8,128)(2,1)}, u32[]{:S(2)}) copy-start(bf16[1024,256]{1,0:T(8,128)(2,1)} %c_ref.11) | copy-start | bytes 1572868
  41.4 11.1 %collective-permute-start = (bf16[1024,256]{1,0:T(8,128)(2,1)S(1)}, bf16[1024,256]{1,0:T(8,128)(2,1)S(1)}, u32[]{:S(2)}, u32[]{:S(2)}) collective-permute-start(bf16[1024,256]{1,0:T(8,128)(2,1)S(1)} %bitcast.10), channel_id=1, source_target_pairs={{0,16},{64,65},{1,17},{65,66},{2,18},{66,67},{3,19},{67,68},{4,20}... | collective-permute-start | bytes 1572872 | tf_op jit(solution)/shard_map/ppermute | solution.py:252
  44.7 10.2 %collective-permute-start.2 = (bf16[1024,256]{1,0:T(8,128)(2,1)S(1)}, bf16[1024,256]{1,0:T(8,128)(2,1)S(1)}, u32[]{:S(2)}, u32[]{:S(2)}) collective-permute-start(bf16[1024,256]{1,0:T(8,128)(2,1)S(1)} %bitcast.11), channel_id=1, source_target_pairs={{0,48},{64,79},{1,49},{65,64},{2,50},{66,65},{3,51},{67,66},{4,52}... | collective-permute-start | bytes 1572872 | tf_op jit(solution)/shard_map/ppermute | solution.py:253
  47.9 12.0 %collective-permute-start.1 = (bf16[1024,256]{1,0:T(8,128)(2,1)S(1)}, bf16[1024,256]{1,0:T(8,128)(2,1)S(1)}, u32[]{:S(2)}, u32[]{:S(2)}) collective-permute-start(bf16[1024,256]{1,0:T(8,128)(2,1)S(1)} %bitcast.12), channel_id=1, source_target_pairs={{0,32},{64,66},{1,33},{65,79},{2,34},{66,68},{3,35},{67,65},{4,36}... | collective-permute-start | bytes 1572872 | tf_op jit(solution)/shard_map/ppermute | solution.py:251
  59.9 1.4 %copy-start.2 = (bf16[1024,256]{1,0:T(8,128)(2,1)}, bf16[1024,256]{1,0:T(8,128)(2,1)S(1)}, u32[]{:S(2)}) copy-start(bf16[1024,256]{1,0:T(8,128)(2,1)S(1)} %collective-permute-done.1.r2_ref.r2) | copy-start | bytes 1572868
  68.2 20.5 %copy-start.3 = (bf16[1024,256]{1,0:T(8,128)(2,1)S(1)}, bf16[1024,256]{1,0:T(8,128)(2,1)}, u32[]{:S(2)}) copy-start(bf16[1024,256]{1,0:T(8,128)(2,1)} %copy-done.2) | copy-start | bytes 1572868
  68.9 19.7 %all-to-all-start.3 = ((f32[16,32,128]{2,1,0:T(8,128)}), f32[16,32,128]{2,1,0:T(8,128)S(1)}, u32[]{:S(2)}, u32[]{:S(2)}) async-start(f32[16,32,128]{2,1,0:T(8,128)} %merge.1), calls=%async_computation.3 | async-start | bytes 524288 | tf_op jit(solution)/shard_map/all_to_all | solution.py:258
  91.5 15.6 %collective-permute-start.3 = (f32[4,136,256]{2,1,0:T(8,128)S(1)}, f32[4,136,256]{2,1,0:T(8,128)S(1)}, u32[]{:S(2)}, u32[]{:S(2)}) collective-permute-start(f32[4,136,256]{2,1,0:T(8,128)S(1)} %half_sums.3), channel_id=1, source_target_pairs={{0,64},{64,0},{1,65},{65,1},{2,66},{66,2},{3,67},{67,3},{4,68},{68... | collective-permute-start | bytes 1671176 | tf_op jit(solution)/shard_map/ppermute | solution.py:237
  103.1 1.0 copy-start.4
  107.1 11.4 %collective-permute-start.4 = (f32[136,256]{1,0:T(8,128)S(1)}, f32[136,256]{1,0:T(8,128)S(1)}, u32[]{:S(2)}, u32[]{:S(2)}) collective-permute-start(f32[136,256]{1,0:T(8,128)S(1)} %get-tuple-element.9), channel_id=1, source_target_pairs={{0,256},{128,384},{256,0},{384,128},{1,257},{129,385},{257,1},{385... | collective-permute-start | bytes 417800 | tf_op jit(solution)/shard_map/ppermute | solution.py:237
  111.9 8.1 %collective-permute-start.5 = (f32[136,256]{1,0:T(8,128)S(1)}, f32[136,256]{1,0:T(8,128)S(1)}, u32[]{:S(2)}, u32[]{:S(2)}) collective-permute-start(f32[136,256]{1,0:T(8,128)S(1)} %get-tuple-element.10), channel_id=1, source_target_pairs={{0,128},{128,256},{256,384},{384,0},{1,129},{129,257},{257,385},{3... | collective-permute-start | bytes 417800 | tf_op jit(solution)/shard_map/ppermute | solution.py:237
  114.3 6.6 %collective-permute-start.6 = (f32[136,256]{1,0:T(8,128)S(1)}, f32[136,256]{1,0:T(8,128)S(1)}, u32[]{:S(2)}, u32[]{:S(2)}) collective-permute-start(f32[136,256]{1,0:T(8,128)S(1)} %get-tuple-element.11), channel_id=1, source_target_pairs={{0,384},{128,0},{256,128},{384,256},{1,385},{129,1},{257,129},{385... | collective-permute-start | bytes 417800 | tf_op jit(solution)/shard_map/ppermute | solution.py:237

commit v3 on v2

--- a/solution.py
+++ b/solution.py
@@ -9,6 +9,7 @@
 
 WIDTH = 256
 SUB = 256
+STEP = 512
 LANES = 128
 F32 = jnp.float32
 BF16 = jnp.bfloat16
@@ -22,9 +23,9 @@
 
 
 def mixed_groups():
-    along_z = [[place(0, x, 4 * h + i) for i in range(4)] for x in range(4) for h in range(4)]
-    along_x = [[place(1, i, z) for i in range(4)] for z in range(16)]
-    return along_z + along_x
+    along_x = [[place(0, i, z) for i in range(4)] for z in range(16)]
+    along_z = [[place(1, x, 4 * h + i) for i in range(4)] for x in range(4) for h in range(4)]
+    return along_x + along_z
 
 
 def mixed_moves(d):
@@ -32,8 +33,8 @@
     for x in range(4):
         for z in range(16):
             dz = -d if d == 2 and z % 2 else d
-            moves.append((place(0, x, z), place(0, (x + d) % 4, z)))
-            moves.append((place(1, x, z), place(1, x, (z + dz) % 16)))
+            moves.append((place(0, x, z), place(0, x, (z + dz) % 16)))
+            moves.append((place(1, x, z), place(1, (x + d) % 4, z)))
     return moves
 
 
@@ -91,7 +92,7 @@
     return pl.multiple_of(((me + 4 - d) % 4) * 8, 8)
 
 
-def last_kernel(me_ref, r2_ref, c_ref, l0_ref, l1_ref, l3_ref, out_ref, cs_ref, hn_ref):
+def last_kernel(me_ref, core_ref, y_ref, r2_ref, c_ref, l0_ref, l1_ref, l3_ref, out_ref, cs_ref, hn_ref):
     l2 = piece_stats(r2_ref, c_ref, cs_ref, hn_ref)
     pieces = (l0_ref[...], l1_ref[...], l2, l3_ref[...])
     me = me_ref[0]
@@ -100,18 +101,18 @@
             out_ref[copy, pl.ds(piece_at(me, d), 8), :] = pieces[d]
 
 
-def last_stats(me, r2, centers, l0, l1, l3, copies):
+def last_stats(ids, r2, centers, l0, l1, l3, copies):
     n = 4 * r2.shape[0]
     smem, vmem = pl.BlockSpec(memory_space=pltpu.SMEM), pl.BlockSpec(memory_space=pltpu.VMEM)
     return pl.pallas_call(
         last_kernel,
-        in_specs=[smem] + [vmem] * 5,
+        in_specs=[smem] * 3 + [vmem] * 5,
         out_shape=jax.ShapeDtypeStruct((copies, n // LANES, LANES), F32),
         scratch_shapes=center_scratch(centers.shape[0]),
         compiler_params=PARAMS,
         cost_estimate=cost(r2.shape[0], centers.shape[0], 1),
         name="last_stats",
-    )(me, r2, centers, l0, l1, l3)
+    )(*ids, r2, centers, l0, l1, l3)
 
 
 def merged(parts_ref):
@@ -137,17 +138,17 @@
     )(parts)
 
 
-def sums_kernel(parts, me_ref, half_ref, r0, r1, r2, r3, c_ref, parts_ref, out_ref, mass_ref, l_ref, cs_ref, hn_ref):
+def sums_kernel(parts, other, me_ref, core_ref, r0, r1, r2, r3, c_ref, parts_ref, out_ref, mass_ref, l_ref, cs_ref, hn_ref):
     half, k = out_ref.shape[0] * (out_ref.shape[1] - 8), out_ref.shape[1] - 8
-    start = pl.multiple_of(half_ref[0] * half, half)
+    start = pl.multiple_of((1 - core_ref[0] if other else core_ref[0]) * half, half)
     cs_ref[...], hn_ref[...] = prepared(c_ref[pl.ds(start, half), :])
-    me, n = me_ref[0], SUB // LANES
+    me, n = me_ref[0], STEP // LANES
     l_ref[...] = merged(parts_ref)
     first = True
     for d, ref in enumerate((r0, r1, r2, r3)):
         piece = l_ref[pl.ds(piece_at(me, d), 8), :]
-        for j in range(ref.shape[0] // SUB):
-            rows = ref[j * SUB : (j + 1) * SUB, :]
+        for j in range(ref.shape[0] // STEP):
+            rows = ref[j * STEP : (j + 1) * STEP, :]
             at = j * n
             lse = jnp.concatenate([piece[at + i : at + i + 1, :] for i in range(n)], axis=1)
             resp = jnp.exp(scores(cs_ref[...], hn_ref[...], rows) - lse)
@@ -168,64 +169,89 @@
     out_ref[:, k:, :] = jnp.zeros((parts, 8, WIDTH), F32)
     for p in range(parts):
         mass = jnp.sum(jnp.transpose(mass_ref[p * k : (p + 1) * k, :]), axis=0, keepdims=True)
-        lane = (p % 2) * LANES
-        for q in range(parts):
-            out_ref[q, k + p // 2 : k + p // 2 + 1, lane : lane + LANES] = mass
-        out_ref[p, k + 2 : k + 3, :LANES] = mass
-
-
-def half_sums(me, half, pieces, centers, stats, parts):
+        out_ref[p, k : k + 1, :LANES] = mass
+
+
+def half_sums(ids, other, pieces, centers, stats, parts):
     k = centers.shape[0] // 2
     l = stats.shape[1:]
     smem, vmem = pl.BlockSpec(memory_space=pltpu.SMEM), pl.BlockSpec(memory_space=pltpu.VMEM)
     return pl.pallas_call(
-        functools.partial(sums_kernel, parts),
+        functools.partial(sums_kernel, parts, other),
         in_specs=[smem] * 2 + [vmem] * 6,
         out_shape=jax.ShapeDtypeStruct((parts, k // parts + 8, WIDTH), F32),
         scratch_shapes=[pltpu.VMEM((k, LANES), F32), pltpu.VMEM(l, F32)] + center_scratch(k),
         compiler_params=PARAMS,
         cost_estimate=cost(l[0] * LANES, k, 2),
         name="half_sums",
-    )(me, half, *pieces, centers, stats)
-
-
-def combine_kernel(y_ref, a_ref, b_ref, *out_refs):
-    for d, out_ref in enumerate(out_refs):
-        p = (y_ref[0] + d) % 4
-        out_ref[...] = a_ref[p] + b_ref[p]
-
-
-def combine(y, a, b):
+    )(*ids[:2], *pieces, centers, stats)
+
+
+def combine_kernel(a_ref, b_ref, out_ref):
+    out_ref[...] = a_ref[...] + b_ref[...]
+
+
+def combine(a, b):
+    return pl.pallas_call(
+        combine_kernel,
+        out_shape=jax.ShapeDtypeStruct(a.shape, F32),
+        compiler_params=PARAMS,
+        name="combine",
+    )(a, b)
+
+
+def finish_kernel(core_ref, y_ref, got_ref, centers_ref, out_ref):
+    k = got_ref.shape[1] - 8
+    centers = centers_ref[pl.ds(pl.multiple_of((core_ref[0] * 4 + y_ref[0]) * k, k), k), :]
+    total = got_ref[0]
+    for i in range(1, got_ref.shape[0]):
+        total = total + got_ref[i]
+    mass = total[k : k + 1, :LANES]
+    own = jnp.transpose(jnp.broadcast_to(mass, (LANES, k)))
+    own = jnp.concatenate([own] * (WIDTH // LANES), axis=1)
+    new = ((total[:k, :] + centers.astype(F32)) / (own + 1.0)).astype(BF16)
+    high = mass.astype(BF16)
+    rest = mass - high.astype(F32)
+    middle = rest.astype(BF16)
+    low = (rest - middle.astype(F32)).astype(BF16)
+    terms = [jnp.concatenate([t.astype(F32)] * (WIDTH // LANES), axis=1) for t in (high, middle, low)]
+    terms = jnp.concatenate(terms + [jnp.zeros((13, WIDTH), F32)], axis=0).astype(BF16)
+    for copy in range(out_ref.shape[0]):
+        out_ref[copy, :k, :] = new
+        out_ref[copy, k:, :] = terms
+
+
+def finish(ids, got, centers, copies):
+    k = got.shape[1] - 8
     smem, vmem = pl.BlockSpec(memory_space=pltpu.SMEM), pl.BlockSpec(memory_space=pltpu.VMEM)
     return pl.pallas_call(
-        combine_kernel,
-        in_specs=[smem, vmem, vmem],
-        out_shape=[jax.ShapeDtypeStruct(a.shape[1:], F32)] * a.shape[0],
-        compiler_params=PARAMS,
-        name="combine",
-    )(y, a, b)
-
-
-def finish_kernel(a_ref, b_ref, c_ref, d_ref, centers_ref, new_ref, mass_ref):
-    k = centers_ref.shape[0]
-    total = (a_ref[...] + b_ref[...]) + (c_ref[...] + d_ref[...])
-    mass_ref[...] = total[k : k + 2, :]
-    own = jnp.transpose(jnp.broadcast_to(total[k + 2 : k + 3, :LANES], (LANES, k)))
-    own = jnp.concatenate([own] * (WIDTH // LANES), axis=1)
-    new_ref[...] = ((total[:k, :] + centers_ref[...].astype(F32)) / (own + 1.0)).astype(BF16)
-
-
-def finish(got, centers):
-    k = centers.shape[0]
-    return pl.pallas_call(
         finish_kernel,
+        in_specs=[smem, smem, vmem, vmem],
+        out_shape=jax.ShapeDtypeStruct((copies, k + 16, WIDTH), BF16),
+        compiler_params=PARAMS,
+        name="finish",
+    )(*ids[1:], got, centers)
+
+
+def split_kernel(parts_ref, new_ref, mass_ref):
+    k = parts_ref.shape[1] - 16
+    for p in range(parts_ref.shape[0]):
+        new_ref[p * k : (p + 1) * k, :] = parts_ref[p, :k, :]
+        terms = parts_ref[p, k:, :LANES].astype(F32)
+        mass_ref[p : p + 1, :] = (terms[0:1] + terms[1:2]) + terms[2:3]
+
+
+def split(parts):
+    n, k = parts.shape[0], parts.shape[1] - 16
+    return pl.pallas_call(
+        split_kernel,
         out_shape=(
-            jax.ShapeDtypeStruct((k, WIDTH), BF16),
-            jax.ShapeDtypeStruct((2, WIDTH), F32),
+            jax.ShapeDtypeStruct((n * k, WIDTH), BF16),
+            jax.ShapeDtypeStruct((n, k), F32),
         ),
         compiler_params=PARAMS,
-        name="finish",
-    )(*got, centers)
+        name="split",
+    )(parts)
 
 
 def everyone(value, axes, count, groups=None):
@@ -238,11 +264,9 @@
 
 
 def body(points, centers, picks):
-    core = lax.axis_index("core").astype(jnp.int32).reshape(1)
-    y = lax.axis_index("y").astype(jnp.int32).reshape(1)
-    me = jnp.where(core == 0, lax.axis_index("x"), lax.axis_index("zl")).astype(jnp.int32)
-    k = centers.shape[0] // 8
-    mine = lax.dynamic_slice_in_dim(centers, (core[0] * 4 + y[0]) * k, k, 0)
+    core = lax.axis_index("core")
+    me = jnp.where(core == 0, lax.axis_index("zl"), lax.axis_index("x"))
+    ids = [i.astype(jnp.int32).reshape(1) for i in (me, core, lax.axis_index("y"))]
 
     chosen = (picks[:, None] == lax.iota(jnp.int32, points.shape[0])[None, :]).astype(BF16)
     rows = jnp.dot(chosen, points, preferred_element_type=F32).astype(BF16)
@@ -253,19 +277,17 @@
     r3 = lax.ppermute(r0, GROUP, mixed_moves(-1))
 
     l0, l1, l3 = row_stats(r0, centers), row_stats(r1, centers), row_stats(r3, centers)
-    stats = last_stats(me, r2, centers, l0, l1, l3, 4)
-    stats = lax.all_to_all(stats, "x", 0, 0, tiled=True)
-    stats = lax.all_to_all(merge(stats, 16), ("zh", "zl"), 0, 0, tiled=True)
+    stats = last_stats(ids, r2, centers, l0, l1, l3, 16)
+    stats = lax.all_to_all(stats, ("x", "zl"), 0, 0, tiled=True)
+    stats = lax.all_to_all(merge(stats, 4), "zh", 0, 0, tiled=True)
 
     pieces = (r0, r1, r2, r3)
-    theirs = half_sums(me, 1 - core, pieces, centers, stats, 4)
+    theirs = half_sums(ids, True, pieces, centers, stats, 4)
     theirs = around(theirs, "core", 2, 1)
-    sums = combine(y, half_sums(me, core, pieces, centers, stats, 4), theirs)
-    got = [sums[0]] + [around(sums[d], "y", 4, d) for d in (2, 1, 3)]
-    new, mass = finish(got, mine)
-    new = lax.all_gather(new, "y", axis=0, tiled=True)
-    new = lax.all_gather(new, "core", axis=0, tiled=True)
-    mass = lax.all_gather(mass, "core", axis=0, tiled=True)
+    sums = combine(half_sums(ids, False, pieces, centers, stats, 4), theirs)
+    got = lax.all_to_all(sums, "y", 0, 0, tiled=True)
+    new = lax.all_to_all(finish(ids, got, centers, 4), "y", 0, 0, tiled=True)
+    new, mass = split(lax.all_gather(new, "core", axis=0, tiled=True))
     return (new, mass.reshape(-1))
 
 

time: 141 us -> 134 us (0.950)
  blocking collectives: 63.6 us -> 95 us
  starting transfers between devices: 39.1 us -> 14.9 us
  waiting for transfers between devices: 20.2 us -> 8.9 us
  local copies, waits for them, and re-layouts: 3.33 us -> 0.89 us
    all_to_all x1 -> x4, blocking collectives: 6.84 us -> 49.9 us  [the longest x1 17.5 us: body(): stats = lax.all_to_all(merge(stats, 4), 'zh', 0, 0, tiled=True)]
    ppermute x4 -> x1, starting transfers between devices: 23 us -> 5.3 us  [around(): lax.ppermute(value, axis, [(i, (i + d) % count) for i in range(count)])]
    all_gather x3 -> x1, blocking collectives: 17.8 us -> 4.39 us  [body(): new, mass = split(lax.all_gather(new, 'core', axis=0, tiled=True))]
    all_to_all x1 -> x0, waiting for transfers between devices: 12.8 us -> none  [body(): stats = lax.all_to_all(merge(stats, 16), ('zh', 'zl'), 0, 0, tiled=True)]
    ppermute x1, waiting for transfers between devices: 0.43 us -> 8.89 us  [body(): r1 = lax.ppermute(r0, GROUP, mixed_moves(1))]
    all_to_all x1 -> x0, starting transfers between devices: 6.94 us -> none  [body(): stats = lax.all_to_all(merge(stats, 16), ('zh', 'zl'), 0, 0, tiled=True)]
    ppermute x1, waiting for transfers between devices: 3.53 us -> 0.01 us  [body(): r2 = lax.ppermute(r0, GROUP, mixed_moves(2))]
    unnamed x12 -> x4, local copies, waits for them, and re-layouts: 3.28 us -> 0.84 us
  transfers between devices with their start and end apart: 8 -> 4, of which waited for: 6 -> 1; matrix products, arithmetic and copies ran while one was open for 0% -> 0% of each run, Pallas kernels for 5% -> 5%
where the time goes in v3:
time: 134 us; the launch traced here: 133 us
  blocking collectives  95 us (71%)
  starting transfers between devices  14.9 us (11%)
  Pallas kernels  11.9 us (9%)
  waiting for transfers between devices  8.9 us (7%)
    all_to_all x2, blocking collectives, everyone(): lax.all_to_all(sent, axes, 0, 0, tiled=True, axis_index_groups=groups)  40.8 us
    all_to_all x1, blocking collectives, body(): stats = lax.all_to_all(merge(stats, 4), 'zh', 0, 0, tiled=True)  17.5 us
    all_to_all x1, blocking collectives, body(): got = lax.all_to_all(sums, 'y', 0, 0, tiled=True)  13.4 us
    all_to_all x1, blocking collectives, body(): stats = lax.all_to_all(stats, ('x', 'zl'), 0, 0, tiled=True)  10.9 us
    ppermute x1, waiting for transfers between devices, body(): r1 = lax.ppermute(r0, GROUP, mixed_moves(1))  8.89 us
    all_to_all x1, blocking collectives, body(): new = lax.all_to_all(finish(ids, got, centers, 4), 'y', 0, 0, tiled=True)  8.07 us
    ppermute x1, starting transfers between devices, around(): lax.ppermute(value, axis, [(i, (i + d) % count) for i in range(count)])  5.3 us
    pallas_call x2, Pallas kernels, half_sums(): pl.pallas_call(functools.partial(sums_kernel, parts, other), in_specs=[sm...  5.05 us
  transfers between devices with their start and end apart: 4, of which 1 were waited for; matrix products, arithmetic and copies ran while one was open for 0% of the time, Pallas kernels for 5%

profile of v3, /device:TPU:1, one launch (start us, length us, event | category | flops | bytes accessed | tf_op | source)
XLA Modules:
  0.0 133.2 jit_solution(18222219051612621549)
XLA Ops:
  0.6 0.0 copy-start
  0.6 0.8 copy-done
  1.5 0.8 convolution_convert_fusion
  2.3 28.1 %all_to_all.30 = bf16[4,64,256]{2,1,0:T(8,128)(2,1)S(1)} all-to-all(bf16[4,64,256]{2,1,0:T(8,128)(2,1)S(1)} %broadcast_in_dim.6), channel_id=1, replica_groups=mesh['y'=4,'core'=2,'x'=4,'zh'=4,'zl'=4] {'zh'}, dimensions={0} | all-to-all | bytes 262144 | tf_op jit(solution)/shard_map/all_to_all | solution.py:259
  30.5 0.0 copy-start.1
  30.5 12.7 %all_to_all.31 = bf16[4,256,256]{2,1,0:T(8,128)(2,1)S(1)} all-to-all(bf16[4,256,256]{2,1,0:T(8,128)(2,1)S(1)} %broadcast_in_dim.8), channel_id=1, replica_groups={{0,16,32,48},{1,17,33,49},{2,18,34,50},{3,19,35,51},{4,20,36,52},{5,21,..., dimensions={0} | all-to-all | bytes 1048576 | tf_op jit(solution)/shard_map/all_to_all | solution.py:259
  43.2 4.4 %collective-permute-start.2 = (bf16[1024,256]{1,0:T(8,128)(2,1)S(1)}, bf16[1024,256]{1,0:T(8,128)(2,1)S(1)}, u32[]{:S(2)}, u32[]{:S(2)}) collective-permute-start(bf16[1024,256]{1,0:T(8,128)(2,1)S(1)} %bitcast.7), channel_id=1, source_target_pairs={{0,15},{64,112},{1,0},{65,113},{2,1},{66,114},{3,2},{67,115},{4,3}... | collective-permute-start | bytes 1572872 | tf_op jit(solution)/shard_map/ppermute | solution.py:277
  47.5 1.9 %collective-permute-start = (bf16[1024,256]{1,0:T(8,128)(2,1)S(1)}, bf16[1024,256]{1,0:T(8,128)(2,1)S(1)}, u32[]{:S(2)}, u32[]{:S(2)}) collective-permute-start(bf16[1024,256]{1,0:T(8,128)(2,1)S(1)} %bitcast.8), channel_id=1, source_target_pairs={{0,1},{64,80},{1,2},{65,81},{2,3},{66,82},{3,4},{67,83},{4,5},{68,... | collective-permute-start | bytes 1572872 | tf_op jit(solution)/shard_map/ppermute | solution.py:276
  49.5 3.3 %collective-permute-start.1 = (bf16[1024,256]{1,0:T(8,128)(2,1)S(1)}, bf16[1024,256]{1,0:T(8,128)(2,1)S(1)}, u32[]{:S(2)}, u32[]{:S(2)}) collective-permute-start(bf16[1024,256]{1,0:T(8,128)(2,1)S(1)} %bitcast.9), channel_id=1, source_target_pairs={{0,2},{64,96},{1,15},{65,97},{2,4},{66,98},{3,1},{67,99},{4,6},{68... | collective-permute-start | bytes 1572872 | tf_op jit(solution)/shard_map/ppermute | solution.py:275
  52.8 0.0 copy-done.1
  52.8 1.4 %row_stats.3.l0_ref = f32[8,128]{1,0:T(8,128)S(1)} custom-call(bf16[1024,256]{1,0:T(8,128)(2,1)S(1)} %bitcast.10, bf16[1024,256]{1,0:T(8,128)(2,1)S(1)} %copy-done.1), custom_call_target="tpu_custom_call" | custom-call | flops 536870912 | bytes 1048576 | tf_op jit(solution)/shard_map/row_stats/pallas_call | solution.py:81
  54.3 0.0 collective-permute-done.2.rows_ref.r3
  54.3 1.4 %row_stats.5.l3_ref = f32[8,128]{1,0:T(8,128)S(1)} custom-call(bf16[1024,256]{1,0:T(8,128)(2,1)S(1)} %collective-permute-done.2.rows_ref.r3, bf16[1024,256]{1,0:T(8,128)(2,1)S(1)} %copy-done.1), custom_call_target="tpu_custom_call" | custom-call | flops 536870912 | bytes 1048576 | tf_op jit(solution)/shard_map/row_stats/pallas_call | solution.py:81
  55.7 8.9 %collective-permute-done.rows_ref.r1 = bf16[1024,256]{1,0:T(8,128)(2,1)S(1)} collective-permute-done((bf16[1024,256]{1,0:T(8,128)(2,1)S(1)}, bf16[1024,256]{1,0:T(8,128)(2,1)S(1)}, u32[]{:S(2)}, u32[]{:S(2)}) %collective-permute-start) | collective-permute-done | bytes 524320 | tf_op jit(solution)/shard_map/ppermute | solution.py:276
  64.6 1.4 %row_stats.4.l1_ref = f32[8,128]{1,0:T(8,128)S(1)} custom-call(bf16[1024,256]{1,0:T(8,128)(2,1)S(1)} %collective-permute-done.rows_ref.r1, bf16[1024,256]{1,0:T(8,128)(2,1)S(1)} %copy-done.1), custom_call_target="tpu_custom_call" | custom-call | flops 536870912 | bytes 1048576 | tf_op jit(solution)/shard_map/row_stats/pallas_call | solution.py:81
  66.0 0.0 collective-permute-done.1.r2_ref.r2
  66.0 1.5 %last_stats.1 = f32[16,32,128]{2,1,0:T(8,128)S(1)} custom-call(s32[1]{0:T(128)} %bitcast.2.me_ref, s32[1]{0:T(128)} %bitcast.core_ref, s32[1]{0:T(128)} %bitcast.1.y_ref, bf16[1024,256]{1,0:T(8,128)(2,1)S(1)} %collective-permute-done.1.r2_ref.r2, bf16[1024,256]{1,0:T(8,128)(2,1)S(1)} %copy-done.1, f32[8,128]{1,0:T(8,128)S(1)} %row_stats.3.l0_ref, ...), custom_call_target="tpu_custom_call" | custom-call | flops 536870912 | bytes 1048576 | tf_op jit(solution)/shard_map/last_stats/pallas_call | solution.py:107
  67.5 10.9 %all_to_all.32.parts_ref = f32[16,32,128]{2,1,0:T(8,128)S(1)} all-to-all(f32[16,32,128]{2,1,0:T(8,128)S(1)} %last_stats.1), channel_id=1, replica_groups=mesh['y'=4,'core'=2,'x'=4,'zh'=4,'zl'=4] {'x','zl'}, dimensions={0} | all-to-all | bytes 524288 | tf_op jit(solution)/shard_map/all_to_all | solution.py:281
  78.4 0.1 merge.1
  78.5 17.5 %all_to_all.33.parts_ref = f32[4,32,128]{2,1,0:T(8,128)S(1)} all-to-all(f32[4,32,128]{2,1,0:T(8,128)S(1)} %merge.1), channel_id=1, replica_groups=mesh['y'=4,'core'=2,'x'=4,'zh'=4,'zl'=4] {'zh'}, dimensions={0} | all-to-all | bytes 131072 | tf_op jit(solution)/shard_map/all_to_all | solution.py:282
  96.0 2.5 %half_sums.3 = f32[4,136,256]{2,1,0:T(8,128)S(1)} custom-call(s32[1]{0:T(128)} %bitcast.2.me_ref, s32[1]{0:T(128)} %bitcast.core_ref, bf16[1024,256]{1,0:T(8,128)(2,1)S(1)} %bitcast.11, bf16[1024,256]{1,0:T(8,128)(2,1)S(1)} %collective-permute-done.rows_ref.r1, bf16[1024,256]{1,0:T(8,128)(2,1)S(1)} %collective-permute-done.1.r2_ref.r2, ...), custom_call_target="tpu_custom_call" | custom-call | flops 2147483648 | bytes 2359296 | tf_op jit(solution)/shard_map/half_sums/pallas_call | solution.py:179
  98.5 5.3 %collective-permute-start.3 = (f32[4,136,256]{2,1,0:T(8,128)S(1)}, f32[4,136,256]{2,1,0:T(8,128)S(1)}, u32[]{:S(2)}, u32[]{:S(2)}) collective-permute-start(f32[4,136,256]{2,1,0:T(8,128)S(1)} %half_sums.3), channel_id=1, source_target_pairs={{0,64},{64,0},{1,65},{65,1},{2,66},{66,2},{3,67},{67,3},{4,68},{68... | collective-permute-start | bytes 1671176 | tf_op jit(solution)/shard_map/ppermute | solution.py:263
  103.8 2.5 %half_sums.2.a_ref = f32[4,136,256]{2,1,0:T(8,128)S(1)} custom-call(s32[1]{0:T(128)} %bitcast.2.me_ref, s32[1]{0:T(128)} %bitcast.core_ref, bf16[1024,256]{1,0:T(8,128)(2,1)S(1)} %bitcast.12, bf16[1024,256]{1,0:T(8,128)(2,1)S(1)} %collective-permute-done.rows_ref.r1, bf16[1024,256]{1,0:T(8,128)(2,1)S(1)} %collective-permute-done.1.r2_ref.r2, ...), custom_call_target="tpu_custom_call" | custom-call | flops 2147483648 | bytes 2359296 | tf_op jit(solution)/shard_map/half_sums/pallas_call | solution.py:179
  106.4 0.0 collective-permute-done.3.b_ref
  106.4 0.1 combine.1
  106.4 13.4 %all_to_all.34.got_ref = f32[4,136,256]{2,1,0:T(8,128)S(1)} all-to-all(f32[4,136,256]{2,1,0:T(8,128)S(1)} %combine.1), channel_id=1, replica_groups=mesh['y'=4,'core'=2,'x'=4,'zh'=4,'zl'=4] {'y'}, dimensions={0} | all-to-all | bytes 1114112 | tf_op jit(solution)/shard_map/all_to_all | solution.py:288
  119.8 0.1 finish.1
  119.9 8.1 %all_to_all.35 = bf16[4,144,256]{2,1,0:T(8,128)(2,1)S(1)} all-to-all(bf16[4,144,256]{2,1,0:T(8,128)(2,1)S(1)} %finish.1), channel_id=1, replica_groups=mesh['y'=4,'core'=2,'x'=4,'zh'=4,'zl'=4] {'y'}, dimensions={0} | all-to-all | bytes 589824 | tf_op jit(solution)/shard_map/all_to_all | solution.py:289
  128.0 4.4 %all_gather.3.parts_ref = bf16[8,144,256]{2,1,0:T(8,128)(2,1)S(1)} all-gather(bf16[4,144,256]{2,1,0:T(8,128)(2,1)S(1)} %all_to_all.35), channel_id=1, replica_groups=mesh['y'=4,'core'=2,'x'=4,'zh'=4,'zl'=4] {'core'}, dimensions={0}, use_global_device_ids=true | all-gather | bytes 884736 | tf_op jit(solution)/shard_map/all_gather | solution.py:290
  132.4 0.8 split.1
  (2 shorter events, 0.0 us)
Async XLA Ops:
  0.6 0.8 copy-start
  30.5 22.4 %copy-start.1 = (bf16[1024,256]{1,0:T(8,128)(2,1)S(1)}, bf16[1024,256]{1,0:T(8,128)(2,1)}, u32[]{:S(2)}) copy-start(bf16[1024,256]{1,0:T(8,128)(2,1)} %centers_ref.1) | copy-start | bytes 1572868
  43.2 11.1 %collective-permute-start.2 = (bf16[1024,256]{1,0:T(8,128)(2,1)S(1)}, bf16[1024,256]{1,0:T(8,128)(2,1)S(1)}, u32[]{:S(2)}, u32[]{:S(2)}) collective-permute-start(bf16[1024,256]{1,0:T(8,128)(2,1)S(1)} %bitcast.7), channel_id=1, source_target_pairs={{0,15},{64,112},{1,0},{65,113},{2,1},{66,114},{3,2},{67,115},{4,3}... | collective-permute-start | bytes 1572872 | tf_op jit(solution)/shard_map/ppermute | solution.py:277
  47.5 17.0 %collective-permute-start = (bf16[1024,256]{1,0:T(8,128)(2,1)S(1)}, bf16[1024,256]{1,0:T(8,128)(2,1)S(1)}, u32[]{:S(2)}, u32[]{:S(2)}) collective-permute-start(bf16[1024,256]{1,0:T(8,128)(2,1)S(1)} %bitcast.8), channel_id=1, source_target_pairs={{0,1},{64,80},{1,2},{65,81},{2,3},{66,82},{3,4},{67,83},{4,5},{68,... | collective-permute-start | bytes 1572872 | tf_op jit(solution)/shard_map/ppermute | solution.py:276
  49.5 16.6 %collective-permute-start.1 = (bf16[1024,256]{1,0:T(8,128)(2,1)S(1)}, bf16[1024,256]{1,0:T(8,128)(2,1)S(1)}, u32[]{:S(2)}, u32[]{:S(2)}) collective-permute-start(bf16[1024,256]{1,0:T(8,128)(2,1)S(1)} %bitcast.9), channel_id=1, source_target_pairs={{0,2},{64,96},{1,15},{65,97},{2,4},{66,98},{3,1},{67,99},{4,6},{68... | collective-permute-start | bytes 1572872 | tf_op jit(solution)/shard_map/ppermute | solution.py:275
  98.5 7.8 %collective-permute-start.3 = (f32[4,136,256]{2,1,0:T(8,128)S(1)}, f32[4,136,256]{2,1,0:T(8,128)S(1)}, u32[]{:S(2)}, u32[]{:S(2)}) collective-permute-start(f32[4,136,256]{2,1,0:T(8,128)S(1)} %half_sums.3), channel_id=1, source_target_pairs={{0,64},{64,0},{1,65},{65,1},{2,66},{66,2},{3,67},{67,3},{4,68},{68... | collective-permute-start | bytes 1671176 | tf_op jit(solution)/shard_map/ppermute | solution.py:263

commit v4 on v3

--- a/solution.py
+++ b/solution.py
@@ -22,20 +22,27 @@
     return (core * 4 + x) * 16 + z
 
 
-def mixed_groups():
-    along_x = [[place(0, i, z) for i in range(4)] for z in range(16)]
-    along_z = [[place(1, x, 4 * h + i) for i in range(4)] for x in range(4) for h in range(4)]
+def mixed_groups(first):
+    c = first
+    along_x = [[place(c, i, z) for i in range(4)] for z in range(16)]
+    along_z = [[place(1 - c, x, 4 * h + i) for i in range(4)] for x in range(4) for h in range(4)]
     return along_x + along_z
 
 
-def mixed_moves(d):
-    moves = []
+def far_groups():
+    core0 = [[place(0, x, z) for z in range(16)] for x in range(4)]
+    core1 = [[place(1, x, 4 * h + i) for x in range(4) for h in range(4)] for i in range(4)]
+    return core0 + core1
+
+
+def swaps(step):
+    out = []
     for x in range(4):
         for z in range(16):
-            dz = -d if d == 2 and z % 2 else d
-            moves.append((place(0, x, z), place(0, x, (z + dz) % 16)))
-            moves.append((place(1, x, z), place(1, (x + d) % 4, z)))
-    return moves
+            near = z ^ 1 if step == 0 else (z + 1 if z % 2 else z - 1) % 16
+            out.append((place(0, x, z), place(0, x ^ 1 if step == 0 else 3 - x, z)))
+            out.append((place(1, x, z), place(1, x, near)))
+    return out
 
 
 def cost(rows, centers, dots):
@@ -57,62 +64,50 @@
     return dots - jnp.concatenate([hn] * (rows.shape[0] // LANES), axis=1)
 
 
-def piece_stats(rows_ref, c_ref, cs_ref, hn_ref):
-    cs_ref[...], hn_ref[...] = prepared(c_ref[...])
-    out = []
-    for j in range(rows_ref.shape[0] // SUB):
-        s = scores(cs_ref[...], hn_ref[...], rows_ref[j * SUB : (j + 1) * SUB, :])
-        top = jnp.max(s, axis=0, keepdims=True)
-        lse = top + jnp.log(jnp.sum(jnp.exp(s - top), axis=0, keepdims=True))
-        out += [lse[:, i * LANES : (i + 1) * LANES] for i in range(SUB // LANES)]
-    return jnp.concatenate(out, axis=0)
-
-
 def center_scratch(k):
     return [pltpu.VMEM((k, WIDTH), BF16), pltpu.VMEM((k, LANES), F32)]
 
 
-def stats_kernel(rows_ref, c_ref, l_ref, cs_ref, hn_ref):
-    l_ref[...] = piece_stats(rows_ref, c_ref, cs_ref, hn_ref)
-
-
-def row_stats(rows, centers):
-    n, k = rows.shape[0], centers.shape[0]
+def stats_kernel(me_ref, core_ref, y_ref, rows_ref, *refs):
+    *chunks, out_ref, cs_ref, hn_ref = refs
+    before_ref = chunks.pop(0).at[0] if len(chunks[0].shape) == 3 else None
+    k = cs_ref.shape[0] // 2
+    if len(chunks) == 1:
+        chunks = [chunks[0].at[:k], chunks[0].at[k:]]
+    for p, chunk in enumerate(chunks):
+        cs_ref[p * k : (p + 1) * k, :], hn_ref[p * k : (p + 1) * k, :] = prepared(chunk[...])
+    for j in range(rows_ref.shape[0] // SUB):
+        rows = rows_ref[j * SUB : (j + 1) * SUB, :]
+        tops, totals = [], []
+        for p in range(len(chunks)):
+            s = scores(cs_ref[p * k : (p + 1) * k, :], hn_ref[p * k : (p + 1) * k, :], rows)
+            tops.append(jnp.max(s, axis=0, keepdims=True))
+            totals.append(jnp.sum(jnp.exp(s - tops[-1]), axis=0, keepdims=True))
+        n = SUB // LANES
+        if before_ref is not None:
+            tops.append(jnp.concatenate([before_ref[j * n + i : j * n + i + 1, :] for i in range(n)], axis=1))
+            totals.append(jnp.ones_like(tops[-1]))
+        top = functools.reduce(jnp.maximum, tops)
+        lse = top + jnp.log(sum(c * jnp.exp(t - top) for c, t in zip(totals, tops)))
+        for i in range(n):
+            at = j * n + i
+            row = lse[:, i * LANES : (i + 1) * LANES]
+            for copy in range(out_ref.shape[0]):
+                out_ref[copy, at : at + 1, :] = row
+
+
+def row_stats(ids, rows, chunks, copies):
+    n, k = rows.shape[0], 2 * chunks[0].shape[0] if len(chunks) == 2 and chunks[0].shape == chunks[1].shape else chunks[-1].shape[0]
+    smem, vmem = pl.BlockSpec(memory_space=pltpu.SMEM), pl.BlockSpec(memory_space=pltpu.VMEM)
     return pl.pallas_call(
         stats_kernel,
-        out_shape=jax.ShapeDtypeStruct((n // LANES, LANES), F32),
+        in_specs=[smem] * 3 + [vmem] * (1 + len(chunks)),
+        out_shape=jax.ShapeDtypeStruct((copies, n // LANES, LANES), F32),
         scratch_shapes=center_scratch(k),
         compiler_params=PARAMS,
         cost_estimate=cost(n, k, 1),
         name="row_stats",
-    )(rows, centers)
-
-
-def piece_at(me, d):
-    return pl.multiple_of(((me + 4 - d) % 4) * 8, 8)
-
-
-def last_kernel(me_ref, core_ref, y_ref, r2_ref, c_ref, l0_ref, l1_ref, l3_ref, out_ref, cs_ref, hn_ref):
-    l2 = piece_stats(r2_ref, c_ref, cs_ref, hn_ref)
-    pieces = (l0_ref[...], l1_ref[...], l2, l3_ref[...])
-    me = me_ref[0]
-    for copy in range(out_ref.shape[0]):
-        for d in range(4):
-            out_ref[copy, pl.ds(piece_at(me, d), 8), :] = pieces[d]
-
-
-def last_stats(ids, r2, centers, l0, l1, l3, copies):
-    n = 4 * r2.shape[0]
-    smem, vmem = pl.BlockSpec(memory_space=pltpu.SMEM), pl.BlockSpec(memory_space=pltpu.VMEM)
-    return pl.pallas_call(
-        last_kernel,
-        in_specs=[smem] * 3 + [vmem] * 5,
-        out_shape=jax.ShapeDtypeStruct((copies, n // LANES, LANES), F32),
-        scratch_shapes=center_scratch(centers.shape[0]),
-        compiler_params=PARAMS,
-        cost_estimate=cost(r2.shape[0], centers.shape[0], 1),
-        name="last_stats",
-    )(*ids, r2, centers, l0, l1, l3)
+    )(*ids, rows, *chunks)
 
 
 def merged(parts_ref):
@@ -138,19 +133,24 @@
     )(parts)
 
 
-def sums_kernel(parts, other, me_ref, core_ref, r0, r1, r2, r3, c_ref, parts_ref, out_ref, mass_ref, l_ref, cs_ref, hn_ref):
+def sums_kernel(parts, other, me_ref, core_ref, r0, r1, r2, c_ref, lse_ref, out_ref, mass_ref, cs_ref, hn_ref):
     half, k = out_ref.shape[0] * (out_ref.shape[1] - 8), out_ref.shape[1] - 8
     start = pl.multiple_of((1 - core_ref[0] if other else core_ref[0]) * half, half)
     cs_ref[...], hn_ref[...] = prepared(c_ref[pl.ds(start, half), :])
-    me, n = me_ref[0], STEP // LANES
-    l_ref[...] = merged(parts_ref)
+    me, n, m = me_ref[0], STEP // LANES, r0.shape[0]
+    flipped = 3 - me
+    blocks = (
+        (r0, me),
+        (r1, me + 1 - 2 * (me % 2)),
+        (r2.at[:m], flipped),
+        (r2.at[m:], flipped + 1 - 2 * (flipped % 2)),
+    )
     first = True
-    for d, ref in enumerate((r0, r1, r2, r3)):
-        piece = l_ref[pl.ds(piece_at(me, d), 8), :]
-        for j in range(ref.shape[0] // STEP):
+    for ref, fourth in blocks:
+        piece = lse_ref[pl.ds(pl.multiple_of(fourth * 8, 8), 8), :]
+        for j in range(m // STEP):
             rows = ref[j * STEP : (j + 1) * STEP, :]
-            at = j * n
-            lse = jnp.concatenate([piece[at + i : at + i + 1, :] for i in range(n)], axis=1)
+            lse = jnp.concatenate([piece[j * n + i : j * n + i + 1, :] for i in range(n)], axis=1)
             resp = jnp.exp(scores(cs_ref[...], hn_ref[...], rows) - lse)
             mass = resp[:, :LANES]
             for i in range(1, n):
@@ -172,19 +172,18 @@
         out_ref[p, k : k + 1, :LANES] = mass
 
 
-def half_sums(ids, other, pieces, centers, stats, parts):
+def half_sums(ids, other, blocks, centers, lse, parts):
     k = centers.shape[0] // 2
-    l = stats.shape[1:]
     smem, vmem = pl.BlockSpec(memory_space=pltpu.SMEM), pl.BlockSpec(memory_space=pltpu.VMEM)
     return pl.pallas_call(
         functools.partial(sums_kernel, parts, other),
-        in_specs=[smem] * 2 + [vmem] * 6,
+        in_specs=[smem] * 2 + [vmem] * 5,
         out_shape=jax.ShapeDtypeStruct((parts, k // parts + 8, WIDTH), F32),
-        scratch_shapes=[pltpu.VMEM((k, LANES), F32), pltpu.VMEM(l, F32)] + center_scratch(k),
-        compiler_params=PARAMS,
-        cost_estimate=cost(l[0] * LANES, k, 2),
+        scratch_shapes=[pltpu.VMEM((k, LANES), F32)] + center_scratch(k),
+        compiler_params=PARAMS,
+        cost_estimate=cost(lse.shape[0] * LANES, k, 2),
         name="half_sums",
-    )(*ids[:2], *pieces, centers, stats)
+    )(*ids[:2], *blocks, centers, lse)
 
 
 def combine_kernel(a_ref, b_ref, out_ref):
@@ -263,28 +262,70 @@
     return lax.ppermute(value, axis, [(i, (i + d) % count) for i in range(count)])
 
 
+def pair_kernel(a_ref, b_ref, after_ref, pair_ref):
+    k = a_ref.shape[0]
+    pair_ref[:k, :] = a_ref[...]
+    pair_ref[k:, :] = b_ref[...]
+
+
+def pair_after(a, b, after):
+    k = a.shape[0]
+    vmem = pl.BlockSpec(memory_space=pltpu.VMEM)
+    return pl.pallas_call(
+        pair_kernel,
+        in_specs=[vmem, vmem, pl.BlockSpec(memory_space=pl.ANY)],
+        out_shape=jax.ShapeDtypeStruct((2 * k, WIDTH), BF16),
+        compiler_params=PARAMS,
+        name="pair_after",
+    )(a, b, after)
+
+
+def near_kernel(rows_ref, a_ref, b_ref, sent_ref, pair_ref):
+    k = a_ref.shape[0]
+    for copy in range(sent_ref.shape[0]):
+        sent_ref[copy] = rows_ref[...]
+    pair_ref[:k, :] = a_ref[...]
+    pair_ref[k:, :] = b_ref[...]
+
+
+def copies_and_pair(rows, a, b, copies):
+    k = a.shape[0]
+    return pl.pallas_call(
+        near_kernel,
+        out_shape=(
+            jax.ShapeDtypeStruct((copies,) + rows.shape, BF16),
+            jax.ShapeDtypeStruct((2 * k, WIDTH), BF16),
+        ),
+        compiler_params=PARAMS,
+        name="copies_and_pair",
+    )(rows, a, b)
+
+
 def body(points, centers, picks):
     core = lax.axis_index("core")
-    me = jnp.where(core == 0, lax.axis_index("zl"), lax.axis_index("x"))
+    me = jnp.where(core == 0, lax.axis_index("x"), lax.axis_index("zl"))
     ids = [i.astype(jnp.int32).reshape(1) for i in (me, core, lax.axis_index("y"))]
 
+    near = lax.ppermute(centers, GROUP, swaps(0))
     chosen = (picks[:, None] == lax.iota(jnp.int32, points.shape[0])[None, :]).astype(BF16)
     rows = jnp.dot(chosen, points, preferred_element_type=F32).astype(BF16)
     rows = everyone(rows, "zh", 4).reshape(-1, WIDTH)
-    r0 = everyone(rows, GROUP, 4, mixed_groups()).reshape(-1, WIDTH)
-    r2 = lax.ppermute(r0, GROUP, mixed_moves(2))
-    r1 = lax.ppermute(r0, GROUP, mixed_moves(1))
-    r3 = lax.ppermute(r0, GROUP, mixed_moves(-1))
-
-    l0, l1, l3 = row_stats(r0, centers), row_stats(r1, centers), row_stats(r3, centers)
-    stats = last_stats(ids, r2, centers, l0, l1, l3, 16)
-    stats = lax.all_to_all(stats, ("x", "zl"), 0, 0, tiled=True)
-    stats = lax.all_to_all(merge(stats, 4), "zh", 0, 0, tiled=True)
-
-    pieces = (r0, r1, r2, r3)
-    theirs = half_sums(ids, True, pieces, centers, stats, 4)
+    rows, pair = copies_and_pair(rows, centers, near, 4)
+    across = lax.ppermute(pair, GROUP, swaps(1))
+    rows = lax.all_to_all(rows, GROUP, 0, 0, tiled=True, axis_index_groups=mixed_groups(1)).reshape(-1, WIDTH)
+    next_rows = lax.ppermute(rows, GROUP, swaps(0))
+
+    stats = row_stats(ids, rows, (centers, near), 1)
+    stats = row_stats(ids, rows, (stats, across), 16)
+    pair = pair_after(rows, next_rows, stats)
+    stats = lax.all_to_all(stats, GROUP, 0, 0, tiled=True, axis_index_groups=far_groups())
+    blocks = rows, next_rows, lax.ppermute(pair, GROUP, swaps(1))
+    stats = merge(stats, 4)
+    lse = lax.all_to_all(stats, GROUP, 0, 0, tiled=True, axis_index_groups=mixed_groups(0)).reshape(-1, LANES)
+
+    theirs = half_sums(ids, True, blocks, centers, lse, 4)
     theirs = around(theirs, "core", 2, 1)
-    sums = combine(half_sums(ids, False, pieces, centers, stats, 4), theirs)
+    sums = combine(half_sums(ids, False, blocks, centers, lse, 4), theirs)
     got = lax.all_to_all(sums, "y", 0, 0, tiled=True)
     new = lax.all_to_all(finish(ids, got, centers, 4), "y", 0, 0, tiled=True)
     new, mass = split(lax.all_gather(new, "core", axis=0, tiled=True))

time: 134 us -> 128 us (0.955)
  blocking collectives: 95 us -> 85.6 us
  starting transfers between devices: 14.9 us -> 17.1 us
  Pallas kernels: 11.9 us -> 13.8 us
    all_to_all x2 -> x1, blocking collectives: 40.8 us -> 26.9 us  [everyone(): lax.all_to_all(sent, axes, 0, 0, tiled=True, axis_index_groups=groups)]
    all_to_all x0 -> x1, waiting for transfers between devices: none -> 5.02 us  [body(): lax.all_to_all(rows, GROUP, 0, 0, tiled=True, axis_index_groups=mixed_gro...]
    all_to_all x2, blocking collectives: 28.4 us -> 32.8 us  [the longest x1 22.9 us: body(): lax.all_to_all(stats, GROUP, 0, 0, tiled=True, axis_index_groups=far_grou...]
    ppermute x3 -> x4, waiting for transfers between devices: 8.9 us -> 4.85 us  [the longest x1 4.84 us: body(): across = lax.ppermute(pair, GROUP, swaps(1))]
    all_to_all x0 -> x1, starting transfers between devices: none -> 3.96 us  [body(): lax.all_to_all(rows, GROUP, 0, 0, tiled=True, axis_index_groups=mixed_gro...]
    ppermute x1, starting transfers between devices: 5.3 us -> 2.1 us  [around(): lax.ppermute(value, axis, [(i, (i + d) % count) for i in range(count)])]
    pallas_call x4, Pallas kernels: 5.74 us -> 7.55 us  [the longest x2 6.59 us: row_stats(): pl.pallas_call(stats_kernel, in_specs=[smem] * 3 + [vmem] * (1 + len(chun...]
    ppermute x3 -> x4, starting transfers between devices: 9.63 us -> 11 us  [the longest x1 4.51 us: body(): near = lax.ppermute(centers, GROUP, swaps(0))]
  transfers between devices with their start and end apart: 4 -> 6, of which waited for: 1 -> 2; matrix products, arithmetic and copies ran while one was open for 0% -> 1% of each run, Pallas kernels for 5% -> 7%
where the time goes in v4:
time: 128 us
  blocking collectives  85.6 us (67%)
  starting transfers between devices  17.1 us (13%)
  Pallas kernels  13.8 us (11%)
  waiting for transfers between devices  9.87 us (8%)
    all_to_all x1, blocking collectives, everyone(): lax.all_to_all(sent, axes, 0, 0, tiled=True, axis_index_groups=groups)  26.9 us
    all_to_all x1, blocking collectives, body(): lax.all_to_all(stats, GROUP, 0, 0, tiled=True, axis_index_groups=far_grou...  22.9 us
    all_to_all x1, blocking collectives, body(): got = lax.all_to_all(sums, 'y', 0, 0, tiled=True)  12.8 us
    all_to_all x1, blocking collectives, body(): lax.all_to_all(stats, GROUP, 0, 0, tiled=True, axis_index_groups=mixed_gr...  9.95 us
    all_to_all x1, blocking collectives, body(): new = lax.all_to_all(finish(ids, got, centers, 4), 'y', 0, 0, tiled=True)  8.07 us
    pallas_call x2, Pallas kernels, row_stats(): pl.pallas_call(stats_kernel, in_specs=[smem] * 3 + [vmem] * (1 + len(chun...  6.59 us
    pallas_call x2, Pallas kernels, half_sums(): pl.pallas_call(functools.partial(sums_kernel, parts, other), in_specs=[sm...  5.15 us
    all_to_all x1, waiting for transfers between devices, body(): lax.all_to_all(rows, GROUP, 0, 0, tiled=True, axis_index_groups=mixed_gro...  5.02 us
  transfers between devices with their start and end apart: 6, of which 2 were waited for; matrix products, arithmetic and copies ran while one was open for 1% of the time, Pallas kernels for 7%

profile of v4, /device:TPU:1, one launch (start us, length us, event | category | flops | bytes accessed | tf_op | source)
XLA Modules:
  0.0 127.9 jit_solution(6432129062867788958)
XLA Ops:
  0.6 0.0 copy-start
  0.6 0.0 copy-start.1
  0.7 4.5 %collective-permute-start = (bf16[1024,256]{1,0:T(8,128)(2,1)}, bf16[1024,256]{1,0:T(8,128)(2,1)S(1)}, u32[]{:S(2)}, u32[]{:S(2)}) collective-permute-start(bf16[1024,256]{1,0:T(8,128)(2,1)} %centers_ref.1), channel_id=1, source_target_pairs={{0,16},{64,65},{1,17},{65,64},{2,18},{66,67},{3,19},{67,66},{4,20}... | collective-permute-start | bytes 1572872 | tf_op jit(solution)/shard_map/ppermute | solution.py:309
  5.2 0.0 copy-done
  5.2 0.8 convolution_convert_fusion
  6.0 26.9 %all_to_all.30 = bf16[4,64,256]{2,1,0:T(8,128)(2,1)S(1)} all-to-all(bf16[4,64,256]{2,1,0:T(8,128)(2,1)S(1)} %broadcast_in_dim.2), channel_id=1, replica_groups=mesh['y'=4,'core'=2,'x'=4,'zh'=4,'zl'=4] {'zh'}, dimensions={0} | all-to-all | bytes 262144 | tf_op jit(solution)/shard_map/all_to_all | solution.py:258
  32.9 0.0 collective-permute-done.b_ref.refs_1_
  32.9 0.0 copy-done.1
  32.9 0.9 copies_and_pair.1
  33.8 4.0 %all-to-all-start.1 = ((bf16[4,256,256]{2,1,0:T(8,128)(2,1)}), bf16[4,256,256]{2,1,0:T(8,128)(2,1)S(1)}, u32[]{:S(2)}, u32[]{:S(2)}) async-start(bf16[4,256,256]{2,1,0:T(8,128)(2,1)} %get-tuple-element.6), calls=%async_computation.1 | async-start | bytes 1048576 | tf_op jit(solution)/shard_map/all_to_all | solution.py:315
  37.8 1.9 %collective-permute-start.2 = (bf16[2048,256]{1,0:T(8,128)(2,1)S(1)}, bf16[2048,256]{1,0:T(8,128)(2,1)}, u32[]{:S(2)}, u32[]{:S(2)}) collective-permute-start(bf16[2048,256]{1,0:T(8,128)(2,1)S(1)} %get-tuple-element.7), channel_id=1, source_target_pairs={{0,48},{64,79},{1,49},{65,66},{2,50},{66,65},{3,51},{67,68},{4,52}... | collective-permute-start | bytes 3145736 | tf_op jit(solution)/shard_map/ppermute | solution.py:314
  39.7 5.0 %all-to-all-done.1 = bf16[4,256,256]{2,1,0:T(8,128)(2,1)S(1)} async-done(((bf16[4,256,256]{2,1,0:T(8,128)(2,1)}), bf16[4,256,256]{2,1,0:T(8,128)(2,1)S(1)}, u32[]{:S(2)}, u32[]{:S(2)}) %all-to-all-start.1) | async-done | bytes 524320 | tf_op jit(solution)/shard_map/all_to_all | solution.py:315
  44.7 2.7 %collective-permute-start.1 = (bf16[1024,256]{1,0:T(8,128)(2,1)S(1)}, bf16[1024,256]{1,0:T(8,128)(2,1)S(1)}, u32[]{:S(2)}, u32[]{:S(2)}) collective-permute-start(bf16[1024,256]{1,0:T(8,128)(2,1)S(1)} %bitcast.8), channel_id=1, source_target_pairs={{0,16},{64,65},{1,17},{65,64},{2,18},{66,67},{3,19},{67,66},{4,20}... | collective-permute-start | bytes 1572872 | tf_op jit(solution)/shard_map/ppermute | solution.py:316
  47.4 2.7 %row_stats.2.refs_0_ = f32[1,8,128]{2,1,0:T(8,128)S(1)} custom-call(s32[1]{0:T(128)} %bitcast.2.me_ref, s32[1]{0:T(128)} %bitcast.core_ref, s32[1]{0:T(128)} %bitcast.1.y_ref, bf16[1024,256]{1,0:T(8,128)(2,1)S(1)} %bitcast.9, bf16[1024,256]{1,0:T(8,128)(2,1)S(1)} %copy-done.1, bf16[1024,256]{1,0:T(8,128)(2,1)S(1)} %collective-permute-done.b_ref.refs_1_), custom_call_target="tpu_custom_call" | custom-call | flops 1073741824 | bytes 1572864 | tf_op jit(solution)/shard_map/row_stats/pallas_call | solution.py:102
  50.1 4.8 %collective-permute-done.2.refs_1_ = bf16[2048,256]{1,0:T(8,128)(2,1)} collective-permute-done((bf16[2048,256]{1,0:T(8,128)(2,1)S(1)}, bf16[2048,256]{1,0:T(8,128)(2,1)}, u32[]{:S(2)}, u32[]{:S(2)}) %collective-permute-start.2) | collective-permute-done | bytes 1048608 | tf_op jit(solution)/shard_map/ppermute | solution.py:314
  54.9 3.9 %row_stats.3.after_ref = f32[16,8,128]{2,1,0:T(8,128)S(1)} custom-call(s32[1]{0:T(128)} %bitcast.2.me_ref, s32[1]{0:T(128)} %bitcast.core_ref, s32[1]{0:T(128)} %bitcast.1.y_ref, bf16[1024,256]{1,0:T(8,128)(2,1)S(1)} %bitcast.10, f32[1,8,128]{2,1,0:T(8,128)S(1)} %row_stats.2.refs_0_, bf16[2048,256]{1,0:T(8,128)(2,1)} %collective-permute-done.2.refs_1_), custom_call_target="tpu_custom_call" | custom-call | flops 1073741824 | bytes 1572864 | tf_op jit(solution)/shard_map/row_stats/pallas_call | solution.py:102
  58.9 0.0 collective-permute-done.1.b_ref.r1
  58.9 0.1 pair_after.1
  59.0 1.9 %collective-permute-start.3 = (bf16[2048,256]{1,0:T(8,128)(2,1)S(1)}, bf16[2048,256]{1,0:T(8,128)(2,1)S(1)}, u32[]{:S(2)}, u32[]{:S(2)}) collective-permute-start(bf16[2048,256]{1,0:T(8,128)(2,1)S(1)} %pair_after.1), channel_id=1, source_target_pairs={{0,48},{64,79},{1,49},{65,66},{2,50},{66,65},{3,51},{67,68},{4,52}... | collective-permute-start | bytes 3145736 | tf_op jit(solution)/shard_map/ppermute | solution.py:322
  60.9 22.9 %all_to_all.31.parts_ref = f32[16,8,128]{2,1,0:T(8,128)S(1)} all-to-all(f32[16,8,128]{2,1,0:T(8,128)S(1)} %row_stats.3.after_ref), channel_id=1, replica_groups={{0,1,2,3,4,5,6,7,8,9,10,11,12,13,14,15},{16,17,18,19,20,21,22,23,24,25,..., dimensions={0} | all-to-all | bytes 131072 | tf_op jit(solution)/shard_map/all_to_all | solution.py:321
  83.8 9.9 %all_to_all.32 = f32[4,8,128]{2,1,0:T(8,128)S(1)} all-to-all(f32[4,8,128]{2,1,0:T(8,128)S(1)} %merge.1), channel_id=1, replica_groups={{0,16,32,48},{1,17,33,49},{2,18,34,50},{3,19,35,51},{4,20,36,52},{5,21,..., dimensions={0} | all-to-all | bytes 32768 | tf_op jit(solution)/shard_map/all_to_all | solution.py:324
  93.8 0.0 collective-permute-done.3.r2
  93.8 2.6 %half_sums.3 = f32[4,136,256]{2,1,0:T(8,128)S(1)} custom-call(s32[1]{0:T(128)} %bitcast.2.me_ref, s32[1]{0:T(128)} %bitcast.core_ref, bf16[1024,256]{1,0:T(8,128)(2,1)S(1)} %bitcast.12, bf16[1024,256]{1,0:T(8,128)(2,1)S(1)} %collective-permute-done.1.b_ref.r1, bf16[2048,256]{1,0:T(8,128)(2,1)S(1)} %collective-permute-done.3.r2, ...), custom_call_target="tpu_custom_call" | custom-call | flops 2147483648 | bytes 2359296 | tf_op jit(solution)/shard_map/half_sums/pallas_call | solution.py:178
  96.3 2.1 %collective-permute-start.4 = (f32[4,136,256]{2,1,0:T(8,128)S(1)}, f32[4,136,256]{2,1,0:T(8,128)S(1)}, u32[]{:S(2)}, u32[]{:S(2)}) collective-permute-start(f32[4,136,256]{2,1,0:T(8,128)S(1)} %half_sums.3), channel_id=1, source_target_pairs={{0,64},{64,0},{1,65},{65,1},{2,66},{66,2},{3,67},{67,3},{4,68},{68... | collective-permute-start | bytes 1671176 | tf_op jit(solution)/shard_map/ppermute | solution.py:262
  98.4 2.6 %half_sums.2.a_ref = f32[4,136,256]{2,1,0:T(8,128)S(1)} custom-call(s32[1]{0:T(128)} %bitcast.2.me_ref, s32[1]{0:T(128)} %bitcast.core_ref, bf16[1024,256]{1,0:T(8,128)(2,1)S(1)} %bitcast.13, bf16[1024,256]{1,0:T(8,128)(2,1)S(1)} %collective-permute-done.1.b_ref.r1, bf16[2048,256]{1,0:T(8,128)(2,1)S(1)} %collective-permute-done.3.r2, ...), custom_call_target="tpu_custom_call" | custom-call | flops 2147483648 | bytes 2359296 | tf_op jit(solution)/shard_map/half_sums/pallas_call | solution.py:178
  101.0 0.0 collective-permute-done.4.b_ref
  101.0 0.1 combine.1
  101.1 12.8 %all_to_all.33.got_ref = f32[4,136,256]{2,1,0:T(8,128)S(1)} all-to-all(f32[4,136,256]{2,1,0:T(8,128)S(1)} %combine.1), channel_id=1, replica_groups=mesh['y'=4,'core'=2,'x'=4,'zh'=4,'zl'=4] {'y'}, dimensions={0} | all-to-all | bytes 1114112 | tf_op jit(solution)/shard_map/all_to_all | solution.py:329
  113.9 0.1 finish.1
  114.0 8.1 %all_to_all.34 = bf16[4,144,256]{2,1,0:T(8,128)(2,1)S(1)} all-to-all(bf16[4,144,256]{2,1,0:T(8,128)(2,1)S(1)} %finish.1), channel_id=1, replica_groups=mesh['y'=4,'core'=2,'x'=4,'zh'=4,'zl'=4] {'y'}, dimensions={0} | all-to-all | bytes 589824 | tf_op jit(solution)/shard_map/all_to_all | solution.py:330
  122.1 5.0 %all_gather.3.parts_ref = bf16[8,144,256]{2,1,0:T(8,128)(2,1)S(1)} all-gather(bf16[4,144,256]{2,1,0:T(8,128)(2,1)S(1)} %all_to_all.34), channel_id=1, replica_groups=mesh['y'=4,'core'=2,'x'=4,'zh'=4,'zl'=4] {'core'}, dimensions={0}, use_global_device_ids=true | all-gather | bytes 884736 | tf_op jit(solution)/shard_map/all_gather | solution.py:331
  127.1 0.8 split.1
  (2 shorter events, 0.1 us)
Async XLA Ops:
  0.6 4.5 %copy-start = (bf16[128,256]{1,0:T(8,128)(2,1)S(1)}, bf16[128,256]{1,0:T(8,128)(2,1)}, u32[]{:S(2)}) copy-start(bf16[128,256]{1,0:T(8,128)(2,1)} %param.3) | copy-start | bytes 196612
  0.6 32.3 %copy-start.1 = (bf16[1024,256]{1,0:T(8,128)(2,1)S(1)}, bf16[1024,256]{1,0:T(8,128)(2,1)}, u32[]{:S(2)}) copy-start(bf16[1024,256]{1,0:T(8,128)(2,1)} %centers_ref.1) | copy-start | bytes 1572868
  0.7 32.3 %collective-permute-start = (bf16[1024,256]{1,0:T(8,128)(2,1)}, bf16[1024,256]{1,0:T(8,128)(2,1)S(1)}, u32[]{:S(2)}, u32[]{:S(2)}) collective-permute-start(bf16[1024,256]{1,0:T(8,128)(2,1)} %centers_ref.1), channel_id=1, source_target_pairs={{0,16},{64,65},{1,17},{65,64},{2,18},{66,67},{3,19},{67,66},{4,20}... | collective-permute-start | bytes 1572872 | tf_op jit(solution)/shard_map/ppermute | solution.py:309
  33.8 10.9 %all-to-all-start.1 = ((bf16[4,256,256]{2,1,0:T(8,128)(2,1)}), bf16[4,256,256]{2,1,0:T(8,128)(2,1)S(1)}, u32[]{:S(2)}, u32[]{:S(2)}) async-start(bf16[4,256,256]{2,1,0:T(8,128)(2,1)} %get-tuple-element.6), calls=%async_computation.1 | async-start | bytes 1048576 | tf_op jit(solution)/shard_map/all_to_all | solution.py:315
  37.8 17.1 %collective-permute-start.2 = (bf16[2048,256]{1,0:T(8,128)(2,1)S(1)}, bf16[2048,256]{1,0:T(8,128)(2,1)}, u32[]{:S(2)}, u32[]{:S(2)}) collective-permute-start(bf16[2048,256]{1,0:T(8,128)(2,1)S(1)} %get-tuple-element.7), channel_id=1, source_target_pairs={{0,48},{64,79},{1,49},{65,66},{2,50},{66,65},{3,51},{67,68},{4,52}... | collective-permute-start | bytes 3145736 | tf_op jit(solution)/shard_map/ppermute | solution.py:314
  44.7 14.1 %collective-permute-start.1 = (bf16[1024,256]{1,0:T(8,128)(2,1)S(1)}, bf16[1024,256]{1,0:T(8,128)(2,1)S(1)}, u32[]{:S(2)}, u32[]{:S(2)}) collective-permute-start(bf16[1024,256]{1,0:T(8,128)(2,1)S(1)} %bitcast.8), channel_id=1, source_target_pairs={{0,16},{64,65},{1,17},{65,64},{2,18},{66,67},{3,19},{67,66},{4,20}... | collective-permute-start | bytes 1572872 | tf_op jit(solution)/shard_map/ppermute | solution.py:316
  59.0 34.8 %collective-permute-start.3 = (bf16[2048,256]{1,0:T(8,128)(2,1)S(1)}, bf16[2048,256]{1,0:T(8,128)(2,1)S(1)}, u32[]{:S(2)}, u32[]{:S(2)}) collective-permute-start(bf16[2048,256]{1,0:T(8,128)(2,1)S(1)} %pair_after.1), channel_id=1, source_target_pairs={{0,48},{64,79},{1,49},{65,66},{2,50},{66,65},{3,51},{67,68},{4,52}... | collective-permute-start | bytes 3145736 | tf_op jit(solution)/shard_map/ppermute | solution.py:322
  96.3 4.7 %collective-permute-start.4 = (f32[4,136,256]{2,1,0:T(8,128)S(1)}, f32[4,136,256]{2,1,0:T(8,128)S(1)}, u32[]{:S(2)}, u32[]{:S(2)}) collective-permute-start(f32[4,136,256]{2,1,0:T(8,128)S(1)} %half_sums.3), channel_id=1, source_target_pairs={{0,64},{64,0},{1,65},{65,1},{2,66},{66,2},{3,67},{67,3},{4,68},{68... | collective-permute-start | bytes 1671176 | tf_op jit(solution)/shard_map/ppermute | solution.py:262

commit v5 on v4

--- a/solution.py
+++ b/solution.py
@@ -39,8 +39,8 @@
     out = []
     for x in range(4):
         for z in range(16):
-            near = z ^ 1 if step == 0 else (z + 1 if z % 2 else z - 1) % 16
-            out.append((place(0, x, z), place(0, x ^ 1 if step == 0 else 3 - x, z)))
+            near = (z + 1 if z % 2 else z - 1) % 16 if step else z ^ 1
+            out.append((place(0, x, z), place(0, 3 - x if step else x ^ 1, z)))
             out.append((place(1, x, z), place(1, x, near)))
     return out
 
@@ -68,12 +68,10 @@
     return [pltpu.VMEM((k, WIDTH), BF16), pltpu.VMEM((k, LANES), F32)]
 
 
-def stats_kernel(me_ref, core_ref, y_ref, rows_ref, *refs):
+def stats_kernel(chained, me_ref, core_ref, y_ref, rows_ref, *refs):
     *chunks, out_ref, cs_ref, hn_ref = refs
-    before_ref = chunks.pop(0).at[0] if len(chunks[0].shape) == 3 else None
-    k = cs_ref.shape[0] // 2
-    if len(chunks) == 1:
-        chunks = [chunks[0].at[:k], chunks[0].at[k:]]
+    before_ref = chunks.pop(0) if chained else None
+    k = chunks[0].shape[0]
     for p, chunk in enumerate(chunks):
         cs_ref[p * k : (p + 1) * k, :], hn_ref[p * k : (p + 1) * k, :] = prepared(chunk[...])
     for j in range(rows_ref.shape[0] // SUB):
@@ -84,8 +82,8 @@
             tops.append(jnp.max(s, axis=0, keepdims=True))
             totals.append(jnp.sum(jnp.exp(s - tops[-1]), axis=0, keepdims=True))
         n = SUB // LANES
-        if before_ref is not None:
-            tops.append(jnp.concatenate([before_ref[j * n + i : j * n + i + 1, :] for i in range(n)], axis=1))
+        if chained:
+            tops.append(jnp.concatenate([before_ref[0, j * n + i : j * n + i + 1, :] for i in range(n)], axis=1))
             totals.append(jnp.ones_like(tops[-1]))
         top = functools.reduce(jnp.maximum, tops)
         lse = top + jnp.log(sum(c * jnp.exp(t - top) for c, t in zip(totals, tops)))
@@ -96,18 +94,18 @@
                 out_ref[copy, at : at + 1, :] = row
 
 
-def row_stats(ids, rows, chunks, copies):
-    n, k = rows.shape[0], 2 * chunks[0].shape[0] if len(chunks) == 2 and chunks[0].shape == chunks[1].shape else chunks[-1].shape[0]
+def row_stats(ids, rows, before, chunks, copies=1):
+    n, k = rows.shape[0], sum(c.shape[0] for c in chunks)
     smem, vmem = pl.BlockSpec(memory_space=pltpu.SMEM), pl.BlockSpec(memory_space=pltpu.VMEM)
     return pl.pallas_call(
-        stats_kernel,
-        in_specs=[smem] * 3 + [vmem] * (1 + len(chunks)),
+        functools.partial(stats_kernel, bool(before)),
+        in_specs=[smem] * 3 + [vmem] * (1 + len(before) + len(chunks)),
         out_shape=jax.ShapeDtypeStruct((copies, n // LANES, LANES), F32),
         scratch_shapes=center_scratch(k),
         compiler_params=PARAMS,
         cost_estimate=cost(n, k, 1),
         name="row_stats",
-    )(*ids, rows, *chunks)
+    )(*ids, rows, *before, *chunks)
 
 
 def merged(parts_ref):
@@ -138,13 +136,8 @@
     start = pl.multiple_of((1 - core_ref[0] if other else core_ref[0]) * half, half)
     cs_ref[...], hn_ref[...] = prepared(c_ref[pl.ds(start, half), :])
     me, n, m = me_ref[0], STEP // LANES, r0.shape[0]
-    flipped = 3 - me
-    blocks = (
-        (r0, me),
-        (r1, me + 1 - 2 * (me % 2)),
-        (r2.at[:m], flipped),
-        (r2.at[m:], flipped + 1 - 2 * (flipped % 2)),
-    )
+    beside = me + 1 - 2 * (me % 2)
+    blocks = ((r0, me), (r1, beside), (r2.at[:m], 3 - me), (r2.at[m:], 3 - beside))
     first = True
     for ref, fourth in blocks:
         piece = lse_ref[pl.ds(pl.multiple_of(fourth * 8, 8), 8), :]
@@ -280,25 +273,20 @@
     )(a, b, after)
 
 
-def near_kernel(rows_ref, a_ref, b_ref, sent_ref, pair_ref):
-    k = a_ref.shape[0]
-    for copy in range(sent_ref.shape[0]):
-        sent_ref[copy] = rows_ref[...]
-    pair_ref[:k, :] = a_ref[...]
-    pair_ref[k:, :] = b_ref[...]
-
-
-def copies_and_pair(rows, a, b, copies):
-    k = a.shape[0]
-    return pl.pallas_call(
-        near_kernel,
-        out_shape=(
-            jax.ShapeDtypeStruct((copies,) + rows.shape, BF16),
-            jax.ShapeDtypeStruct((2 * k, WIDTH), BF16),
-        ),
-        compiler_params=PARAMS,
-        name="copies_and_pair",
-    )(rows, a, b)
+def copies_kernel(rows_ref, *refs):
+    for copy in range(refs[-1].shape[0]):
+        refs[-1][copy] = rows_ref[...]
+
+
+def copies_after(rows, after, copies):
+    vmem = pl.BlockSpec(memory_space=pltpu.VMEM)
+    return pl.pallas_call(
+        copies_kernel,
+        in_specs=[vmem] + [pl.BlockSpec(memory_space=pl.ANY)] * len(after),
+        out_shape=jax.ShapeDtypeStruct((copies,) + rows.shape, BF16),
+        compiler_params=PARAMS,
+        name="copies",
+    )(rows, *after)
 
 
 def body(points, centers, picks):
@@ -310,13 +298,14 @@
     chosen = (picks[:, None] == lax.iota(jnp.int32, points.shape[0])[None, :]).astype(BF16)
     rows = jnp.dot(chosen, points, preferred_element_type=F32).astype(BF16)
     rows = everyone(rows, "zh", 4).reshape(-1, WIDTH)
-    rows, pair = copies_and_pair(rows, centers, near, 4)
-    across = lax.ppermute(pair, GROUP, swaps(1))
+    across = [lax.ppermute(c, GROUP, swaps(1)) for c in (centers, near)]
+    rows = copies_after(rows, (near,), 4)
     rows = lax.all_to_all(rows, GROUP, 0, 0, tiled=True, axis_index_groups=mixed_groups(1)).reshape(-1, WIDTH)
     next_rows = lax.ppermute(rows, GROUP, swaps(0))
 
-    stats = row_stats(ids, rows, (centers, near), 1)
-    stats = row_stats(ids, rows, (stats, across), 16)
+    stats = row_stats(ids, rows, (), (centers, near))
+    stats = row_stats(ids, rows, (stats,), across[:1])
+    stats = row_stats(ids, rows, (stats,), across[1:], 16)
     pair = pair_after(rows, next_rows, stats)
     stats = lax.all_to_all(stats, GROUP, 0, 0, tiled=True, axis_index_groups=far_groups())
     blocks = rows, next_rows, lax.ppermute(pair, GROUP, swaps(1))

time: 128 us -> 128 us (level)
  starting transfers between devices: 17.1 us -> 23.8 us
  waiting for transfers between devices: 9.87 us -> 3.79 us
    all_to_all x1, waiting for transfers between devices: 5.02 us -> 0.43 us  [body(): lax.all_to_all(rows, GROUP, 0, 0, tiled=True, axis_index_groups=mixed_gro...]
    ppermute x1 -> x2, starting transfers between devices: 1.91 us -> 6.48 us  [body(): across = [lax.ppermute(c, GROUP, swaps(1)) for c in (centers, near)]]
    ppermute x1, starting transfers between devices: 2.1 us -> 3.79 us  [around(): lax.ppermute(value, axis, [(i, (i + d) % count) for i in range(count)])]
    ppermute x1 -> x2, waiting for transfers between devices: 4.84 us -> 3.3 us  [body(): across = [lax.ppermute(c, GROUP, swaps(1)) for c in (centers, near)]]
    pallas_call x3 -> x4, Pallas kernels: 7.48 us -> 6.39 us  [the longest x3 5.56 us: row_stats(): pl.pallas_call(functools.partial(stats_kernel, bool(before)), in_specs=[s...]
  transfers between devices with their start and end apart: 6 -> 7, of which waited for: 2 -> 2; matrix products, arithmetic and copies ran while one was open for 1% -> 1% of each run, Pallas kernels for 7% -> 6%
where the time goes in v5:
time: 128 us
  blocking collectives  85.7 us (67%)
  starting transfers between devices  23.8 us (19%)
  Pallas kernels  12.7 us (10%)
  waiting for transfers between devices  3.79 us (3%)
    all_to_all x1, blocking collectives, everyone(): lax.all_to_all(sent, axes, 0, 0, tiled=True, axis_index_groups=groups)  26.9 us
    all_to_all x1, blocking collectives, body(): lax.all_to_all(stats, GROUP, 0, 0, tiled=True, axis_index_groups=far_grou...  22.6 us
    all_to_all x1, blocking collectives, body(): got = lax.all_to_all(sums, 'y', 0, 0, tiled=True)  13.4 us
    all_to_all x1, blocking collectives, body(): lax.all_to_all(stats, GROUP, 0, 0, tiled=True, axis_index_groups=mixed_gr...  10.4 us
    all_to_all x1, blocking collectives, body(): new = lax.all_to_all(finish(ids, got, centers, 4), 'y', 0, 0, tiled=True)  8.07 us
    ppermute x2, starting transfers between devices, body(): across = [lax.ppermute(c, GROUP, swaps(1)) for c in (centers, near)]  6.48 us
    pallas_call x3, Pallas kernels, row_stats(): pl.pallas_call(functools.partial(stats_kernel, bool(before)), in_specs=[s...  5.56 us
    pallas_call x2, Pallas kernels, half_sums(): pl.pallas_call(functools.partial(sums_kernel, parts, other), in_specs=[sm...  5.14 us
  transfers between devices with their start and end apart: 7, of which 2 were waited for; matrix products, arithmetic and copies ran while one was open for 1% of the time, Pallas kernels for 6%

profile of v5, /device:TPU:1, one launch (start us, length us, event | category | flops | bytes accessed | tf_op | source)
XLA Modules:
  0.0 127.5 jit_solution(15597061682876177457)
XLA Ops:
  0.6 0.0 copy-start
  0.6 4.5 %collective-permute-start = (bf16[1024,256]{1,0:T(8,128)(2,1)}, bf16[1024,256]{1,0:T(8,128)(2,1)S(1)}, u32[]{:S(2)}, u32[]{:S(2)}) collective-permute-start(bf16[1024,256]{1,0:T(8,128)(2,1)} %centers_ref.1), channel_id=1, source_target_pairs={{0,16},{64,65},{1,17},{65,64},{2,18},{66,67},{3,19},{67,66},{4,20}... | collective-permute-start | bytes 1572872 | tf_op jit(solution)/shard_map/ppermute | solution.py:297
  5.2 0.0 copy-done
  5.2 0.8 convolution_convert_fusion
  6.0 26.9 %all_to_all.30 = bf16[4,64,256]{2,1,0:T(8,128)(2,1)S(1)} all-to-all(bf16[4,64,256]{2,1,0:T(8,128)(2,1)S(1)} %broadcast_in_dim.2), channel_id=1, replica_groups=mesh['y'=4,'core'=2,'x'=4,'zh'=4,'zl'=4] {'zh'}, dimensions={0} | all-to-all | bytes 262144 | tf_op jit(solution)/shard_map/all_to_all | solution.py:251
  32.9 0.0 collective-permute-done.refs_0_.refs_1_
  32.9 0.8 copies.1
  33.8 0.0 copy-start.1
  33.8 4.1 %all-to-all-start.1 = ((bf16[4,256,256]{2,1,0:T(8,128)(2,1)}), bf16[4,256,256]{2,1,0:T(8,128)(2,1)S(1)}, u32[]{:S(2)}, u32[]{:S(2)}) async-start(bf16[4,256,256]{2,1,0:T(8,128)(2,1)} %copies.1), calls=%async_computation.1 | async-start | bytes 1048576 | tf_op jit(solution)/shard_map/all_to_all | solution.py:303
  37.9 0.0 copy-done.1
  37.9 1.9 %collective-permute-start.2 = (bf16[1024,256]{1,0:T(8,128)(2,1)S(1)}, bf16[1024,256]{1,0:T(8,128)(2,1)S(1)}, u32[]{:S(2)}, u32[]{:S(2)}) collective-permute-start(bf16[1024,256]{1,0:T(8,128)(2,1)S(1)} %copy-done.1), channel_id=1, source_target_pairs={{0,48},{64,79},{1,49},{65,66},{2,50},{66,65},{3,51},{67,68},{4,52}... | collective-permute-start | bytes 1572872 | tf_op jit(solution)/shard_map/ppermute | solution.py:301
  39.8 4.6 %collective-permute-start.3 = (bf16[1024,256]{1,0:T(8,128)(2,1)S(1)}, bf16[1024,256]{1,0:T(8,128)(2,1)S(1)}, u32[]{:S(2)}, u32[]{:S(2)}) collective-permute-start(bf16[1024,256]{1,0:T(8,128)(2,1)S(1)} %collective-permute-done.refs_0_.refs_1_), channel_id=1, source_target_pairs={{0,48},{64,79},{1,49},{65,66},{2,50},{66,65},{3,51},{67,68},{4,52}... | collective-permute-start | bytes 1572872 | tf_op jit(solution)/shard_map/ppermute | solution.py:301
  44.4 0.4 all-to-all-done.1
  44.8 2.7 %collective-permute-start.1 = (bf16[1024,256]{1,0:T(8,128)(2,1)S(1)}, bf16[1024,256]{1,0:T(8,128)(2,1)S(1)}, u32[]{:S(2)}, u32[]{:S(2)}) collective-permute-start(bf16[1024,256]{1,0:T(8,128)(2,1)S(1)} %bitcast.8), channel_id=1, source_target_pairs={{0,16},{64,65},{1,17},{65,64},{2,18},{66,67},{3,19},{67,66},{4,20}... | collective-permute-start | bytes 1572872 | tf_op jit(solution)/shard_map/ppermute | solution.py:304
  47.5 2.7 %row_stats.3.refs_0_ = f32[1,8,128]{2,1,0:T(8,128)S(1)} custom-call(s32[1]{0:T(128)} %bitcast.2.me_ref, s32[1]{0:T(128)} %bitcast.core_ref, s32[1]{0:T(128)} %bitcast.1.y_ref, bf16[1024,256]{1,0:T(8,128)(2,1)S(1)} %bitcast.9, bf16[1024,256]{1,0:T(8,128)(2,1)S(1)} %copy-done.1, bf16[1024,256]{1,0:T(8,128)(2,1)S(1)} %collective-permute-done.refs_0_.refs_1_), custom_call_target="tpu_custom_call" | custom-call | flops 1073741824 | bytes 1572864 | tf_op jit(solution)/shard_map/row_stats/pallas_call | solution.py:100
  50.1 0.0 collective-permute-done.2.refs_1_
  50.1 1.5 %row_stats.4.refs_0_ = f32[1,8,128]{2,1,0:T(8,128)S(1)} custom-call(s32[1]{0:T(128)} %bitcast.2.me_ref, s32[1]{0:T(128)} %bitcast.core_ref, s32[1]{0:T(128)} %bitcast.1.y_ref, bf16[1024,256]{1,0:T(8,128)(2,1)S(1)} %bitcast.10, f32[1,8,128]{2,1,0:T(8,128)S(1)} %row_stats.3.refs_0_, bf16[1024,256]{1,0:T(8,128)(2,1)S(1)} %collective-permute-done.2.refs_1_), custom_call_target="tpu_custom_call" | custom-call | flops 536870912 | bytes 1048576 | tf_op jit(solution)/shard_map/row_stats/pallas_call | solution.py:100
  51.6 3.3 %collective-permute-done.3.refs_1_ = bf16[1024,256]{1,0:T(8,128)(2,1)S(1)} collective-permute-done((bf16[1024,256]{1,0:T(8,128)(2,1)S(1)}, bf16[1024,256]{1,0:T(8,128)(2,1)S(1)}, u32[]{:S(2)}, u32[]{:S(2)}) %collective-permute-start.3) | collective-permute-done | bytes 524320 | tf_op jit(solution)/shard_map/ppermute | solution.py:301
  54.9 1.5 %row_stats.5.after_ref = f32[16,8,128]{2,1,0:T(8,128)S(1)} custom-call(s32[1]{0:T(128)} %bitcast.2.me_ref, s32[1]{0:T(128)} %bitcast.core_ref, s32[1]{0:T(128)} %bitcast.1.y_ref, bf16[1024,256]{1,0:T(8,128)(2,1)S(1)} %bitcast.11, f32[1,8,128]{2,1,0:T(8,128)S(1)} %row_stats.4.refs_0_, bf16[1024,256]{1,0:T(8,128)(2,1)S(1)} %collective-permute-done.3.refs_1_), custom_call_target="tpu_custom_call" | custom-call | flops 536870912 | bytes 1048576 | tf_op jit(solution)/shard_map/row_stats/pallas_call | solution.py:100
  56.4 0.0 collective-permute-done.1.b_ref.r1
  56.4 0.1 pair_after.1
  56.5 2.2 %collective-permute-start.4 = (bf16[2048,256]{1,0:T(8,128)(2,1)S(1)}, bf16[2048,256]{1,0:T(8,128)(2,1)S(1)}, u32[]{:S(2)}, u32[]{:S(2)}) collective-permute-start(bf16[2048,256]{1,0:T(8,128)(2,1)S(1)} %pair_after.1), channel_id=1, source_target_pairs={{0,48},{64,79},{1,49},{65,66},{2,50},{66,65},{3,51},{67,68},{4,52}... | collective-permute-start | bytes 3145736 | tf_op jit(solution)/shard_map/ppermute | solution.py:311
  58.7 22.6 %all_to_all.31.parts_ref = f32[16,8,128]{2,1,0:T(8,128)S(1)} all-to-all(f32[16,8,128]{2,1,0:T(8,128)S(1)} %row_stats.5.after_ref), channel_id=1, replica_groups={{0,1,2,3,4,5,6,7,8,9,10,11,12,13,14,15},{16,17,18,19,20,21,22,23,24,25,..., dimensions={0} | all-to-all | bytes 131072 | tf_op jit(solution)/shard_map/all_to_all | solution.py:310
  81.3 10.4 %all_to_all.32 = f32[4,8,128]{2,1,0:T(8,128)S(1)} all-to-all(f32[4,8,128]{2,1,0:T(8,128)S(1)} %merge.1), channel_id=1, replica_groups={{0,16,32,48},{1,17,33,49},{2,18,34,50},{3,19,35,51},{4,20,36,52},{5,21,..., dimensions={0} | all-to-all | bytes 32768 | tf_op jit(solution)/shard_map/all_to_all | solution.py:313
  91.7 0.0 collective-permute-done.4.r2
  91.7 2.6 %half_sums.3 = f32[4,136,256]{2,1,0:T(8,128)S(1)} custom-call(s32[1]{0:T(128)} %bitcast.2.me_ref, s32[1]{0:T(128)} %bitcast.core_ref, bf16[1024,256]{1,0:T(8,128)(2,1)S(1)} %bitcast.13, bf16[1024,256]{1,0:T(8,128)(2,1)S(1)} %collective-permute-done.1.b_ref.r1, bf16[2048,256]{1,0:T(8,128)(2,1)S(1)} %collective-permute-done.4.r2, ...), custom_call_target="tpu_custom_call" | custom-call | flops 2147483648 | bytes 2359296 | tf_op jit(solution)/shard_map/half_sums/pallas_call | solution.py:171
  94.3 3.8 %collective-permute-start.5 = (f32[4,136,256]{2,1,0:T(8,128)S(1)}, f32[4,136,256]{2,1,0:T(8,128)S(1)}, u32[]{:S(2)}, u32[]{:S(2)}) collective-permute-start(f32[4,136,256]{2,1,0:T(8,128)S(1)} %half_sums.3), channel_id=1, source_target_pairs={{0,64},{64,0},{1,65},{65,1},{2,66},{66,2},{3,67},{67,3},{4,68},{68... | collective-permute-start | bytes 1671176 | tf_op jit(solution)/shard_map/ppermute | solution.py:255
  98.1 2.6 %half_sums.2.a_ref = f32[4,136,256]{2,1,0:T(8,128)S(1)} custom-call(s32[1]{0:T(128)} %bitcast.2.me_ref, s32[1]{0:T(128)} %bitcast.core_ref, bf16[1024,256]{1,0:T(8,128)(2,1)S(1)} %bitcast.14, bf16[1024,256]{1,0:T(8,128)(2,1)S(1)} %collective-permute-done.1.b_ref.r1, bf16[2048,256]{1,0:T(8,128)(2,1)S(1)} %collective-permute-done.4.r2, ...), custom_call_target="tpu_custom_call" | custom-call | flops 2147483648 | bytes 2359296 | tf_op jit(solution)/shard_map/half_sums/pallas_call | solution.py:171
  100.7 0.0 collective-permute-done.5.b_ref
  100.7 0.1 combine.1
  100.8 13.4 %all_to_all.33.got_ref = f32[4,136,256]{2,1,0:T(8,128)S(1)} all-to-all(f32[4,136,256]{2,1,0:T(8,128)S(1)} %combine.1), channel_id=1, replica_groups=mesh['y'=4,'core'=2,'x'=4,'zh'=4,'zl'=4] {'y'}, dimensions={0} | all-to-all | bytes 1114112 | tf_op jit(solution)/shard_map/all_to_all | solution.py:318
  114.1 0.1 finish.1
  114.2 8.1 %all_to_all.34 = bf16[4,144,256]{2,1,0:T(8,128)(2,1)S(1)} all-to-all(bf16[4,144,256]{2,1,0:T(8,128)(2,1)S(1)} %finish.1), channel_id=1, replica_groups=mesh['y'=4,'core'=2,'x'=4,'zh'=4,'zl'=4] {'y'}, dimensions={0} | all-to-all | bytes 589824 | tf_op jit(solution)/shard_map/all_to_all | solution.py:319
  122.3 4.4 %all_gather.3.parts_ref = bf16[8,144,256]{2,1,0:T(8,128)(2,1)S(1)} all-gather(bf16[4,144,256]{2,1,0:T(8,128)(2,1)S(1)} %all_to_all.34), channel_id=1, replica_groups=mesh['y'=4,'core'=2,'x'=4,'zh'=4,'zl'=4] {'core'}, dimensions={0}, use_global_device_ids=true | all-gather | bytes 884736 | tf_op jit(solution)/shard_map/all_gather | solution.py:320
  126.7 0.8 split.1
  (2 shorter events, 0.1 us)
Async XLA Ops:
  0.6 4.5 %copy-start = (bf16[128,256]{1,0:T(8,128)(2,1)S(1)}, bf16[128,256]{1,0:T(8,128)(2,1)}, u32[]{:S(2)}) copy-start(bf16[128,256]{1,0:T(8,128)(2,1)} %param.3) | copy-start | bytes 196612
  0.6 32.3 %collective-permute-start = (bf16[1024,256]{1,0:T(8,128)(2,1)}, bf16[1024,256]{1,0:T(8,128)(2,1)S(1)}, u32[]{:S(2)}, u32[]{:S(2)}) collective-permute-start(bf16[1024,256]{1,0:T(8,128)(2,1)} %centers_ref.1), channel_id=1, source_target_pairs={{0,16},{64,65},{1,17},{65,64},{2,18},{66,67},{3,19},{67,66},{4,20}... | collective-permute-start | bytes 1572872 | tf_op jit(solution)/shard_map/ppermute | solution.py:297
  33.8 4.1 %copy-start.1 = (bf16[1024,256]{1,0:T(8,128)(2,1)S(1)}, bf16[1024,256]{1,0:T(8,128)(2,1)}, u32[]{:S(2)}) copy-start(bf16[1024,256]{1,0:T(8,128)(2,1)} %centers_ref.1) | copy-start | bytes 1572868
  33.8 11.0 %all-to-all-start.1 = ((bf16[4,256,256]{2,1,0:T(8,128)(2,1)}), bf16[4,256,256]{2,1,0:T(8,128)(2,1)S(1)}, u32[]{:S(2)}, u32[]{:S(2)}) async-start(bf16[4,256,256]{2,1,0:T(8,128)(2,1)} %copies.1), calls=%async_computation.1 | async-start | bytes 1048576 | tf_op jit(solution)/shard_map/all_to_all | solution.py:303
  37.9 12.3 %collective-permute-start.2 = (bf16[1024,256]{1,0:T(8,128)(2,1)S(1)}, bf16[1024,256]{1,0:T(8,128)(2,1)S(1)}, u32[]{:S(2)}, u32[]{:S(2)}) collective-permute-start(bf16[1024,256]{1,0:T(8,128)(2,1)S(1)} %copy-done.1), channel_id=1, source_target_pairs={{0,48},{64,79},{1,49},{65,66},{2,50},{66,65},{3,51},{67,68},{4,52}... | collective-permute-start | bytes 1572872 | tf_op jit(solution)/shard_map/ppermute | solution.py:301
  39.8 15.1 %collective-permute-start.3 = (bf16[1024,256]{1,0:T(8,128)(2,1)S(1)}, bf16[1024,256]{1,0:T(8,128)(2,1)S(1)}, u32[]{:S(2)}, u32[]{:S(2)}) collective-permute-start(bf16[1024,256]{1,0:T(8,128)(2,1)S(1)} %collective-permute-done.refs_0_.refs_1_), channel_id=1, source_target_pairs={{0,48},{64,79},{1,49},{65,66},{2,50},{66,65},{3,51},{67,68},{4,52}... | collective-permute-start | bytes 1572872 | tf_op jit(solution)/shard_map/ppermute | solution.py:301
  44.8 11.6 %collective-permute-start.1 = (bf16[1024,256]{1,0:T(8,128)(2,1)S(1)}, bf16[1024,256]{1,0:T(8,128)(2,1)S(1)}, u32[]{:S(2)}, u32[]{:S(2)}) collective-permute-start(bf16[1024,256]{1,0:T(8,128)(2,1)S(1)} %bitcast.8), channel_id=1, source_target_pairs={{0,16},{64,65},{1,17},{65,64},{2,18},{66,67},{3,19},{67,66},{4,20}... | collective-permute-start | bytes 1572872 | tf_op jit(solution)/shard_map/ppermute | solution.py:304
  56.5 35.3 %collective-permute-start.4 = (bf16[2048,256]{1,0:T(8,128)(2,1)S(1)}, bf16[2048,256]{1,0:T(8,128)(2,1)S(1)}, u32[]{:S(2)}, u32[]{:S(2)}) collective-permute-start(bf16[2048,256]{1,0:T(8,128)(2,1)S(1)} %pair_after.1), channel_id=1, source_target_pairs={{0,48},{64,79},{1,49},{65,66},{2,50},{66,65},{3,51},{67,68},{4,52}... | collective-permute-start | bytes 3145736 | tf_op jit(solution)/shard_map/ppermute | solution.py:311
  94.3 6.4 %collective-permute-start.5 = (f32[4,136,256]{2,1,0:T(8,128)S(1)}, f32[4,136,256]{2,1,0:T(8,128)S(1)}, u32[]{:S(2)}, u32[]{:S(2)}) collective-permute-start(f32[4,136,256]{2,1,0:T(8,128)S(1)} %half_sums.3), channel_id=1, source_target_pairs={{0,64},{64,0},{1,65},{65,1},{2,66},{66,2},{3,67},{67,3},{4,68},{68... | collective-permute-start | bytes 1671176 | tf_op jit(solution)/shard_map/ppermute | solution.py:255

commit v6 on v5

--- a/solution.py
+++ b/solution.py
@@ -127,6 +127,7 @@
         merge_kernel,
         out_shape=jax.ShapeDtypeStruct((copies,) + parts.shape[1:], F32),
         compiler_params=PARAMS,
+        cost_estimate=pl.CostEstimate(flops=12 * 10**9, bytes_accessed=10**6, transcendentals=0),
         name="merge",
     )(parts)
 

time: 128 us -> 126 us (0.984)
  blocking collectives: 85.7 us -> 64 us
  starting transfers between devices: 23.8 us -> 32.6 us
  waiting for transfers between devices: 3.79 us -> 11.6 us
  Pallas kernels: 12.7 us -> 15.6 us
    all_to_all x1 -> x0, blocking collectives: 22.6 us -> none  [body(): lax.all_to_all(stats, GROUP, 0, 0, tiled=True, axis_index_groups=far_grou...]
    all_to_all x0 -> x1, waiting for transfers between devices: none -> 7.89 us  [body(): lax.all_to_all(stats, GROUP, 0, 0, tiled=True, axis_index_groups=far_grou...]
    all_to_all x0 -> x1, starting transfers between devices: none -> 6.6 us  [body(): lax.all_to_all(stats, GROUP, 0, 0, tiled=True, axis_index_groups=far_grou...]
    ppermute x1, starting transfers between devices: 2.23 us -> 5.85 us  [body(): blocks = (rows, next_rows, lax.ppermute(pair, GROUP, swaps(1)))]
    pallas_call x2, Pallas kernels: 5.14 us -> 7.47 us  [half_sums(): pl.pallas_call(functools.partial(sums_kernel, parts, other), in_specs=[sm...]
    ppermute x1, starting transfers between devices: 3.79 us -> 2.36 us  [around(): lax.ppermute(value, axis, [(i, (i + d) % count) for i in range(count)])]
  transfers between devices with their start and end apart: 7 -> 8, of which waited for: 2 -> 3; matrix products, arithmetic and copies ran while one was open for 1% -> 1% of each run, Pallas kernels for 6% -> 8%
where the time goes in v6:
time: 126 us; the launch traced here: 125 us
  blocking collectives  64 us (51%)
  starting transfers between devices  32.6 us (26%)
  Pallas kernels  15.6 us (12%)
  waiting for transfers between devices  11.6 us (9%)
    all_to_all x1, blocking collectives, everyone(): lax.all_to_all(sent, axes, 0, 0, tiled=True, axis_index_groups=groups)  26.9 us
    all_to_all x1, blocking collectives, body(): got = lax.all_to_all(sums, 'y', 0, 0, tiled=True)  13.3 us
    all_to_all x1, blocking collectives, body(): lax.all_to_all(stats, GROUP, 0, 0, tiled=True, axis_index_groups=mixed_gr...  11.3 us
    all_to_all x1, blocking collectives, body(): new = lax.all_to_all(finish(ids, got, centers, 4), 'y', 0, 0, tiled=True)  8.07 us
    all_to_all x1, waiting for transfers between devices, body(): lax.all_to_all(stats, GROUP, 0, 0, tiled=True, axis_index_groups=far_grou...  7.89 us
    pallas_call x2, Pallas kernels, half_sums(): pl.pallas_call(functools.partial(sums_kernel, parts, other), in_specs=[sm...  7.47 us
    all_to_all x1, starting transfers between devices, body(): lax.all_to_all(stats, GROUP, 0, 0, tiled=True, axis_index_groups=far_grou...  6.6 us
    ppermute x2, starting transfers between devices, body(): across = [lax.ppermute(c, GROUP, swaps(1)) for c in (centers, near)]  6.48 us
  transfers between devices with their start and end apart: 8, of which 3 were waited for; matrix products, arithmetic and copies ran while one was open for 1% of the time, Pallas kernels for 8%

profile of v6, /device:TPU:1, one launch (start us, length us, event | category | flops | bytes accessed | tf_op | source)
XLA Modules:
  0.0 125.5 jit_solution(2551328797724303124)
XLA Ops:
  0.6 0.0 copy-start
  0.6 4.5 %collective-permute-start = (bf16[1024,256]{1,0:T(8,128)(2,1)}, bf16[1024,256]{1,0:T(8,128)(2,1)S(1)}, u32[]{:S(2)}, u32[]{:S(2)}) collective-permute-start(bf16[1024,256]{1,0:T(8,128)(2,1)} %centers_ref.1), channel_id=1, source_target_pairs={{0,16},{64,65},{1,17},{65,64},{2,18},{66,67},{3,19},{67,66},{4,20}... | collective-permute-start | bytes 1572872 | tf_op jit(solution)/shard_map/ppermute | solution.py:298
  5.2 0.0 copy-done
  5.2 0.8 convolution_convert_fusion
  6.0 26.9 %all_to_all.30 = bf16[4,64,256]{2,1,0:T(8,128)(2,1)S(1)} all-to-all(bf16[4,64,256]{2,1,0:T(8,128)(2,1)S(1)} %broadcast_in_dim.2), channel_id=1, replica_groups=mesh['y'=4,'core'=2,'x'=4,'zh'=4,'zl'=4] {'zh'}, dimensions={0} | all-to-all | bytes 262144 | tf_op jit(solution)/shard_map/all_to_all | solution.py:252
  32.9 0.0 collective-permute-done.refs_0_.refs_1_
  32.9 0.8 copies.1
  33.8 0.0 copy-start.1
  33.8 4.1 %all-to-all-start.1 = ((bf16[4,256,256]{2,1,0:T(8,128)(2,1)}), bf16[4,256,256]{2,1,0:T(8,128)(2,1)S(1)}, u32[]{:S(2)}, u32[]{:S(2)}) async-start(bf16[4,256,256]{2,1,0:T(8,128)(2,1)} %copies.1), calls=%async_computation.1 | async-start | bytes 1048576 | tf_op jit(solution)/shard_map/all_to_all | solution.py:304
  37.9 0.0 copy-done.1
  37.9 1.9 %collective-permute-start.2 = (bf16[1024,256]{1,0:T(8,128)(2,1)S(1)}, bf16[1024,256]{1,0:T(8,128)(2,1)S(1)}, u32[]{:S(2)}, u32[]{:S(2)}) collective-permute-start(bf16[1024,256]{1,0:T(8,128)(2,1)S(1)} %copy-done.1), channel_id=1, source_target_pairs={{0,48},{64,79},{1,49},{65,66},{2,50},{66,65},{3,51},{67,68},{4,52}... | collective-permute-start | bytes 1572872 | tf_op jit(solution)/shard_map/ppermute | solution.py:302
  39.8 4.6 %collective-permute-start.3 = (bf16[1024,256]{1,0:T(8,128)(2,1)S(1)}, bf16[1024,256]{1,0:T(8,128)(2,1)S(1)}, u32[]{:S(2)}, u32[]{:S(2)}) collective-permute-start(bf16[1024,256]{1,0:T(8,128)(2,1)S(1)} %collective-permute-done.refs_0_.refs_1_), channel_id=1, source_target_pairs={{0,48},{64,79},{1,49},{65,66},{2,50},{66,65},{3,51},{67,68},{4,52}... | collective-permute-start | bytes 1572872 | tf_op jit(solution)/shard_map/ppermute | solution.py:302
  44.4 0.4 all-to-all-done.1
  44.8 2.7 %collective-permute-start.1 = (bf16[1024,256]{1,0:T(8,128)(2,1)S(1)}, bf16[1024,256]{1,0:T(8,128)(2,1)S(1)}, u32[]{:S(2)}, u32[]{:S(2)}) collective-permute-start(bf16[1024,256]{1,0:T(8,128)(2,1)S(1)} %bitcast.8), channel_id=1, source_target_pairs={{0,16},{64,65},{1,17},{65,64},{2,18},{66,67},{3,19},{67,66},{4,20}... | collective-permute-start | bytes 1572872 | tf_op jit(solution)/shard_map/ppermute | solution.py:305
  47.5 2.7 %row_stats.3.refs_0_ = f32[1,8,128]{2,1,0:T(8,128)S(1)} custom-call(s32[1]{0:T(128)} %bitcast.2.me_ref, s32[1]{0:T(128)} %bitcast.core_ref, s32[1]{0:T(128)} %bitcast.1.y_ref, bf16[1024,256]{1,0:T(8,128)(2,1)S(1)} %bitcast.9, bf16[1024,256]{1,0:T(8,128)(2,1)S(1)} %copy-done.1, bf16[1024,256]{1,0:T(8,128)(2,1)S(1)} %collective-permute-done.refs_0_.refs_1_), custom_call_target="tpu_custom_call" | custom-call | flops 1073741824 | bytes 1572864 | tf_op jit(solution)/shard_map/row_stats/pallas_call | solution.py:100
  50.1 0.0 collective-permute-done.2.refs_1_
  50.1 1.5 %row_stats.4.refs_0_ = f32[1,8,128]{2,1,0:T(8,128)S(1)} custom-call(s32[1]{0:T(128)} %bitcast.2.me_ref, s32[1]{0:T(128)} %bitcast.core_ref, s32[1]{0:T(128)} %bitcast.1.y_ref, bf16[1024,256]{1,0:T(8,128)(2,1)S(1)} %bitcast.10, f32[1,8,128]{2,1,0:T(8,128)S(1)} %row_stats.3.refs_0_, bf16[1024,256]{1,0:T(8,128)(2,1)S(1)} %collective-permute-done.2.refs_1_), custom_call_target="tpu_custom_call" | custom-call | flops 536870912 | bytes 1048576 | tf_op jit(solution)/shard_map/row_stats/pallas_call | solution.py:100
  51.6 3.3 %collective-permute-done.3.refs_1_ = bf16[1024,256]{1,0:T(8,128)(2,1)S(1)} collective-permute-done((bf16[1024,256]{1,0:T(8,128)(2,1)S(1)}, bf16[1024,256]{1,0:T(8,128)(2,1)S(1)}, u32[]{:S(2)}, u32[]{:S(2)}) %collective-permute-start.3) | collective-permute-done | bytes 524320 | tf_op jit(solution)/shard_map/ppermute | solution.py:302
  54.9 2.1 %row_stats.5.after_ref = f32[16,8,128]{2,1,0:T(8,128)} custom-call(s32[1]{0:T(128)} %bitcast.2.me_ref, s32[1]{0:T(128)} %bitcast.core_ref, s32[1]{0:T(128)} %bitcast.1.y_ref, bf16[1024,256]{1,0:T(8,128)(2,1)S(1)} %bitcast.11, f32[1,8,128]{2,1,0:T(8,128)S(1)} %row_stats.4.refs_0_, bf16[1024,256]{1,0:T(8,128)(2,1)S(1)} %collective-permute-done.3.refs_1_), custom_call_target="tpu_custom_call" | custom-call | flops 536870912 | bytes 1048576 | tf_op jit(solution)/shard_map/row_stats/pallas_call | solution.py:100
  57.0 6.6 %all-to-all-start.2 = ((f32[16,8,128]{2,1,0:T(8,128)}), f32[16,8,128]{2,1,0:T(8,128)S(1)}, u32[]{:S(2)}, u32[]{:S(2)}) async-start(f32[16,8,128]{2,1,0:T(8,128)} %row_stats.5.after_ref), calls=%async_computation.2 | async-start | bytes 131072 | tf_op jit(solution)/shard_map/all_to_all | solution.py:311
  63.6 0.0 collective-permute-done.1.b_ref.r1
  63.6 0.1 pair_after.1
  63.7 5.9 %collective-permute-start.4 = (bf16[2048,256]{1,0:T(8,128)(2,1)S(1)}, bf16[2048,256]{1,0:T(8,128)(2,1)}, u32[]{:S(2)}, u32[]{:S(2)}) collective-permute-start(bf16[2048,256]{1,0:T(8,128)(2,1)S(1)} %pair_after.1), channel_id=1, source_target_pairs={{0,48},{64,79},{1,49},{65,66},{2,50},{66,65},{3,51},{67,68},{4,52}... | collective-permute-start | bytes 3145736 | tf_op jit(solution)/shard_map/ppermute | solution.py:312
  69.6 7.9 %all-to-all-done.2.parts_ref = f32[16,8,128]{2,1,0:T(8,128)S(1)} async-done(((f32[16,8,128]{2,1,0:T(8,128)}), f32[16,8,128]{2,1,0:T(8,128)S(1)}, u32[]{:S(2)}, u32[]{:S(2)}) %all-to-all-start.2) | async-done | bytes 65568 | tf_op jit(solution)/shard_map/all_to_all | solution.py:311
  77.5 11.3 %all_to_all.31 = f32[4,8,128]{2,1,0:T(8,128)S(1)} all-to-all(f32[4,8,128]{2,1,0:T(8,128)S(1)} %merge.1), channel_id=1, replica_groups={{0,16,32,48},{1,17,33,49},{2,18,34,50},{3,19,35,51},{4,20,36,52},{5,21,..., dimensions={0} | all-to-all | bytes 32768 | tf_op jit(solution)/shard_map/all_to_all | solution.py:314
  88.8 0.0 collective-permute-done.4.r2
  88.8 3.7 %half_sums.3 = f32[4,136,256]{2,1,0:T(8,128)S(1)} custom-call(s32[1]{0:T(128)} %bitcast.2.me_ref, s32[1]{0:T(128)} %bitcast.core_ref, bf16[1024,256]{1,0:T(8,128)(2,1)S(1)} %bitcast.13, bf16[1024,256]{1,0:T(8,128)(2,1)S(1)} %collective-permute-done.1.b_ref.r1, bf16[2048,256]{1,0:T(8,128)(2,1)} %collective-permute-done.4.r2, bf16[1024,256]{1,0:T(8,128)(2,1)S(1)} %copy-done.1, ...), custom_call_target="tpu_custom_call" | custom-call | flops 2147483648 | bytes 2359296 | tf_op jit(solution)/shard_map/half_sums/pallas_call | solution.py:172
  92.6 2.4 %collective-permute-start.5 = (f32[4,136,256]{2,1,0:T(8,128)S(1)}, f32[4,136,256]{2,1,0:T(8,128)S(1)}, u32[]{:S(2)}, u32[]{:S(2)}) collective-permute-start(f32[4,136,256]{2,1,0:T(8,128)S(1)} %half_sums.3), channel_id=1, source_target_pairs={{0,64},{64,0},{1,65},{65,1},{2,66},{66,2},{3,67},{67,3},{4,68},{68... | collective-permute-start | bytes 1671176 | tf_op jit(solution)/shard_map/ppermute | solution.py:256
  94.9 3.7 %half_sums.2.a_ref = f32[4,136,256]{2,1,0:T(8,128)S(1)} custom-call(s32[1]{0:T(128)} %bitcast.2.me_ref, s32[1]{0:T(128)} %bitcast.core_ref, bf16[1024,256]{1,0:T(8,128)(2,1)S(1)} %bitcast.14, bf16[1024,256]{1,0:T(8,128)(2,1)S(1)} %collective-permute-done.1.b_ref.r1, bf16[2048,256]{1,0:T(8,128)(2,1)} %collective-permute-done.4.r2, ...), custom_call_target="tpu_custom_call" | custom-call | flops 2147483648 | bytes 2359296 | tf_op jit(solution)/shard_map/half_sums/pallas_call | solution.py:172
  98.7 0.0 collective-permute-done.5.b_ref
  98.7 0.1 combine.1
  98.7 13.3 %all_to_all.32.got_ref = f32[4,136,256]{2,1,0:T(8,128)S(1)} all-to-all(f32[4,136,256]{2,1,0:T(8,128)S(1)} %combine.1), channel_id=1, replica_groups=mesh['y'=4,'core'=2,'x'=4,'zh'=4,'zl'=4] {'y'}, dimensions={0} | all-to-all | bytes 1114112 | tf_op jit(solution)/shard_map/all_to_all | solution.py:319
  112.0 0.1 finish.1
  112.2 8.1 %all_to_all.33 = bf16[4,144,256]{2,1,0:T(8,128)(2,1)S(1)} all-to-all(bf16[4,144,256]{2,1,0:T(8,128)(2,1)S(1)} %finish.1), channel_id=1, replica_groups=mesh['y'=4,'core'=2,'x'=4,'zh'=4,'zl'=4] {'y'}, dimensions={0} | all-to-all | bytes 589824 | tf_op jit(solution)/shard_map/all_to_all | solution.py:320
  120.2 4.4 %all_gather.3.parts_ref = bf16[8,144,256]{2,1,0:T(8,128)(2,1)S(1)} all-gather(bf16[4,144,256]{2,1,0:T(8,128)(2,1)S(1)} %all_to_all.33), channel_id=1, replica_groups=mesh['y'=4,'core'=2,'x'=4,'zh'=4,'zl'=4] {'core'}, dimensions={0}, use_global_device_ids=true | all-gather | bytes 884736 | tf_op jit(solution)/shard_map/all_gather | solution.py:321
  124.6 0.8 split.1
  (2 shorter events, 0.1 us)
Async XLA Ops:
  0.6 4.5 %copy-start = (bf16[128,256]{1,0:T(8,128)(2,1)S(1)}, bf16[128,256]{1,0:T(8,128)(2,1)}, u32[]{:S(2)}) copy-start(bf16[128,256]{1,0:T(8,128)(2,1)} %param.3) | copy-start | bytes 196612
  0.6 32.3 %collective-permute-start = (bf16[1024,256]{1,0:T(8,128)(2,1)}, bf16[1024,256]{1,0:T(8,128)(2,1)S(1)}, u32[]{:S(2)}, u32[]{:S(2)}) collective-permute-start(bf16[1024,256]{1,0:T(8,128)(2,1)} %centers_ref.1), channel_id=1, source_target_pairs={{0,16},{64,65},{1,17},{65,64},{2,18},{66,67},{3,19},{67,66},{4,20}... | collective-permute-start | bytes 1572872 | tf_op jit(solution)/shard_map/ppermute | solution.py:298
  33.8 4.1 %copy-start.1 = (bf16[1024,256]{1,0:T(8,128)(2,1)S(1)}, bf16[1024,256]{1,0:T(8,128)(2,1)}, u32[]{:S(2)}) copy-start(bf16[1024,256]{1,0:T(8,128)(2,1)} %centers_ref.1) | copy-start | bytes 1572868
  33.8 11.0 %all-to-all-start.1 = ((bf16[4,256,256]{2,1,0:T(8,128)(2,1)}), bf16[4,256,256]{2,1,0:T(8,128)(2,1)S(1)}, u32[]{:S(2)}, u32[]{:S(2)}) async-start(bf16[4,256,256]{2,1,0:T(8,128)(2,1)} %copies.1), calls=%async_computation.1 | async-start | bytes 1048576 | tf_op jit(solution)/shard_map/all_to_all | solution.py:304
  37.9 12.3 %collective-permute-start.2 = (bf16[1024,256]{1,0:T(8,128)(2,1)S(1)}, bf16[1024,256]{1,0:T(8,128)(2,1)S(1)}, u32[]{:S(2)}, u32[]{:S(2)}) collective-permute-start(bf16[1024,256]{1,0:T(8,128)(2,1)S(1)} %copy-done.1), channel_id=1, source_target_pairs={{0,48},{64,79},{1,49},{65,66},{2,50},{66,65},{3,51},{67,68},{4,52}... | collective-permute-start | bytes 1572872 | tf_op jit(solution)/shard_map/ppermute | solution.py:302
  39.8 15.1 %collective-permute-start.3 = (bf16[1024,256]{1,0:T(8,128)(2,1)S(1)}, bf16[1024,256]{1,0:T(8,128)(2,1)S(1)}, u32[]{:S(2)}, u32[]{:S(2)}) collective-permute-start(bf16[1024,256]{1,0:T(8,128)(2,1)S(1)} %collective-permute-done.refs_0_.refs_1_), channel_id=1, source_target_pairs={{0,48},{64,79},{1,49},{65,66},{2,50},{66,65},{3,51},{67,68},{4,52}... | collective-permute-start | bytes 1572872 | tf_op jit(solution)/shard_map/ppermute | solution.py:302
  44.8 18.8 %collective-permute-start.1 = (bf16[1024,256]{1,0:T(8,128)(2,1)S(1)}, bf16[1024,256]{1,0:T(8,128)(2,1)S(1)}, u32[]{:S(2)}, u32[]{:S(2)}) collective-permute-start(bf16[1024,256]{1,0:T(8,128)(2,1)S(1)} %bitcast.8), channel_id=1, source_target_pairs={{0,16},{64,65},{1,17},{65,64},{2,18},{66,67},{3,19},{67,66},{4,20}... | collective-permute-start | bytes 1572872 | tf_op jit(solution)/shard_map/ppermute | solution.py:305
  57.0 20.4 %all-to-all-start.2 = ((f32[16,8,128]{2,1,0:T(8,128)}), f32[16,8,128]{2,1,0:T(8,128)S(1)}, u32[]{:S(2)}, u32[]{:S(2)}) async-start(f32[16,8,128]{2,1,0:T(8,128)} %row_stats.5.after_ref), calls=%async_computation.2 | async-start | bytes 131072 | tf_op jit(solution)/shard_map/all_to_all | solution.py:311
  63.7 25.1 %collective-permute-start.4 = (bf16[2048,256]{1,0:T(8,128)(2,1)S(1)}, bf16[2048,256]{1,0:T(8,128)(2,1)}, u32[]{:S(2)}, u32[]{:S(2)}) collective-permute-start(bf16[2048,256]{1,0:T(8,128)(2,1)S(1)} %pair_after.1), channel_id=1, source_target_pairs={{0,48},{64,79},{1,49},{65,66},{2,50},{66,65},{3,51},{67,68},{4,52}... | collective-permute-start | bytes 3145736 | tf_op jit(solution)/shard_map/ppermute | solution.py:312
  92.6 6.1 %collective-permute-start.5 = (f32[4,136,256]{2,1,0:T(8,128)S(1)}, f32[4,136,256]{2,1,0:T(8,128)S(1)}, u32[]{:S(2)}, u32[]{:S(2)}) collective-permute-start(f32[4,136,256]{2,1,0:T(8,128)S(1)} %half_sums.3), channel_id=1, source_target_pairs={{0,64},{64,0},{1,65},{65,1},{2,66},{66,2},{3,67},{67,3},{4,68},{68... | collective-permute-start | bytes 1671176 | tf_op jit(solution)/shard_map/ppermute | solution.py:256
